TPU v7x, 32 devices: a whole 2x2x4 slice. The times are simulated.
32 devices in a mesh: row: 2 (over x), col: 4 (over y, core), slab: 4 (over z).
Axes of the slice: x: 2, y: 2, z: 4, core: 2. Of those that a mesh axis runs over, the one named last changes fastest.
Arguments:
- inputs: bfloat16 [32, 64, 6144], P('col', None, ('row', 'slab')), may hold values from -6 to 6
- first_weight: bfloat16 [3, 3, 6144, 6144], P(None, None, ('row', 'slab'), 'col'), may hold values from -0.02734375 to 0.02734375
- second_weight: bfloat16 [3, 3, 6144, 6144], P(None, None, 'col', ('row', 'slab')), may hold values from -0.02734375 to 0.02734375
Outputs:
- result: bfloat16 [32, 64, 6144], P('col', None, ('row', 'slab'))
All inputs are finite; a program needn't handle non-finite values.
Results may differ from a plain program's by a relative error of at most 0.015.
Values may be sent and summed in bfloat16 or wider, within the bound.
A program may use at most 192 MiB of HBM per device.

v0:
```python
import jax
import jax.numpy as jnp
from jax import lax
from jax.sharding import PartitionSpec as P


def local(inputs, first_weight, second_weight):
    full_input = lax.all_gather(inputs, "col", axis=0, tiled=True)
    height = full_input.shape[0]
    width = full_input.shape[1]
    pixels = height * width
    out_first = first_weight.shape[3]
    padded = jnp.pad(full_input, ((1, 1), (1, 1), (0, 0)))
    pieces = []
    for vertical in range(3):
        for sideways in range(3):
            window = padded[vertical : vertical + height, sideways : sideways + width, :]
            pieces.append(window.reshape(pixels, full_input.shape[2]))
    columns = jnp.concatenate(pieces, axis=1)
    flat_kernel = first_weight.reshape(9 * first_weight.shape[2], out_first)
    first = lax.psum_scatter(
        jnp.dot(columns, flat_kernel, preferred_element_type=jnp.float32),
        ("row", "slab"),
        scatter_dimension=0,
        tiled=True,
    )
    hidden = jax.nn.silu(first).astype(jnp.bfloat16)
    gathered = lax.all_gather(hidden, ("row", "slab"), axis=0, tiled=True)
    padded_hidden = jnp.pad(gathered.reshape(height, width, out_first), ((1, 1), (1, 1), (0, 0)))
    rows_out = pixels // lax.axis_size("col")
    out_second = second_weight.shape[3]
    lines = rows_out * lax.axis_size("col") // width
    total = jnp.zeros((rows_out * lax.axis_size("col"), out_second), jnp.float32)
    for vertical in range(3):
        for sideways in range(3):
            window = padded_hidden[
                vertical : vertical + lines, sideways : sideways + width, :
            ].reshape(rows_out * lax.axis_size("col"), out_first)
            total = total + jnp.dot(
                window, second_weight[vertical, sideways], preferred_element_type=jnp.float32
            )
    second = lax.psum_scatter(
        total.astype(jnp.bfloat16), "col", scatter_dimension=0, tiled=True
    ).astype(jnp.float32)
    combined = inputs.astype(jnp.float32) + second.reshape(inputs.shape)
    return combined.astype(jnp.bfloat16)


def solution(mesh):
    in_specs = (
        P("col", None, ("row", "slab")),
        P(None, None, ("row", "slab"), "col"),
        P(None, None, "col", ("row", "slab")),
    )
    out_specs = P("col", None, ("row", "slab"))
    return jax.shard_map(local, mesh=mesh, in_specs=in_specs, out_specs=out_specs, check_vma=False)
```

profile of v0, /device:TPU:0, one launch (start us, length us, event | category | flops | bytes accessed | tf_op | source)
XLA Modules:
  0.0 617.6 jit_solution(9250321884872378627)
XLA Ops:
  6.5 0.0 all-gather.3.cloned.1.call-start
  6.5 0.7 all-gather.3.cloned.1.call-update
  7.3 0.0 reduce-scatter.3.cloned.1.call-start
  7.3 32.9 %all-gather.3.cloned.1.call-done = bf16[32,64,768]{2,1,0:T(8,128)(2,1)} async-done(((bf16[8,64,768]{2,1,0:T(8,128)(2,1)}), bf16[32,64,768]{2,1,0:T(8,128)(2,1)}) %all-gather.3.cloned.1.call-update) | async-done | bytes 3145744 | tf_op jit(solution)/shard_map/all_gather | solution.py:8
  40.2 21.5 %pad_slice_fusion.8 = (bf16[32,64,768]{2,1,0:T(8,128)(2,1)S(1)}, bf16[32,64,768]{2,1,0:T(8,128)(2,1)}, bf16[32,64,768]{2,1,0:T(8,128)(2,1)S(1)}, bf16[32,64,768]...) fusion(bf16[32,64,768]{2,1,0:T(8,128)(2,1)} %all-gather.3.clone, ...), kind=kLoop, calls=%fused_computation.9 | loop fusion | bytes 28311552 | tf_op jit(solution)/shard_map/slice | solution.py:17
  61.7 4.0 constant_dynamic-update-slice_fusion.8
  65.6 0.0 copy-done.1
  65.6 1.9 constant_dynamic-update-slice_fusion.7
  67.5 1.9 constant_dynamic-update-slice_fusion.6
  69.5 2.0 constant_dynamic-update-slice_fusion.5
  71.4 0.0 copy-done
  71.4 2.0 constant_dynamic-update-slice_fusion.4
  73.4 2.0 constant_dynamic-update-slice_fusion.3
  75.4 2.0 constant_dynamic-update-slice_fusion.2
  77.5 1.9 constant_dynamic-update-slice_fusion.1
  79.4 1.9 constant_dynamic-update-slice_fusion
  81.3 54.1 %fusion.27 = f32[2048,1536]{1,0:T(8,128)} fusion(bf16[2048,6912]{1,0:T(8,128)(2,1)} %constant_dynamic-update-slice_fusion, bf16[6912,1536]{1,0:T(8,128)(2,1)} %bitcast.92), kind=kOutput, calls=%fused_computation.55 | convolution fusion | flops 43486543872 | bytes 62128128 | tf_op jit(solution)/shard_map/dot_general | solution.py:22
  135.5 0.0 reduce-scatter.3.cloned.1.call-update
  135.5 0.0 all-gather.5.cloned.1.call-start
  135.5 207.4 %reduce-scatter.3.cloned.1.call-done = f32[256,1536]{1,0:T(8,128)} async-done(((f32[2048,1536]{1,0:T(8,128)}), f32[256,1536]{1,0:T(8,128)}) %reduce-scatter.3.cloned.1.call-update) | async-done | bytes 1572880 | tf_op jit(solution)/shard_map/reduce_scatter | solution.py:21
  342.9 2.7 multiply_convert_fusion
  345.6 0.0 all-gather.5.cloned.1.call-update
  345.6 0.0 reduce-scatter.5.cloned.1.call-start
  345.7 98.2 %all-gather.5.cloned.1.call-done = bf16[2048,1536]{1,0:T(8,128)(2,1)} async-done(((bf16[256,1536]{1,0:T(8,128)(2,1)}), bf16[2048,1536]{1,0:T(8,128)(2,1)}) %all-gather.5.cloned.1.call-update) | async-done | bytes 6291472 | tf_op jit(solution)/shard_map/all_gather | solution.py:28
  443.9 37.2 %pad_slice_fusion = (bf16[32,64,1536]{2,1,0:T(8,128)(2,1)}, bf16[32,64,1536]{2,1,0:T(8,128)(2,1)}, bf16[32,64,1536]{2,1,0:T(8,128)(2,1)}, bf16[32,64,1536]{2,1,0...) fusion(bf16[32,64,1536]{2,1,0:T(8,128)(2,1)} %bitcast.71), kind=kLoop, calls=%fused_computation.1 | loop fusion | bytes 56623104 | tf_op jit(solution)/shard_map/slice | solution.py:36
  481.1 0.0 copy-start.2
  481.1 0.0 slice-start.12
  481.1 9.7 %fusion.13 = f32[2048,768]{1,0:T(8,128)} fusion(bf16[2048,1536]{1,0:T(8,128)(2,1)} %bitcast.90, bf16[3,3,1536,768]{3,2,1,0:T(8,128)(2,1)} %param.5), kind=kOutput, calls=%fused_computation.30 | convolution fusion | flops 4831838208 | bytes 14942208 | tf_op jit(solution)/shard_map/dot_general | solution.py:39
  490.8 0.0 copy-done.2
  490.8 8.8 %fusion.11 = f32[2048,768]{1,0:T(8,128)} fusion(bf16[2048,1536]{1,0:T(8,128)(2,1)S(1)} %bitcast.89, bf16[3,3,1536,768]{3,2,1,0:T(8,128)(2,1)} %param.5), kind=kOutput, calls=%fused_computation.28 | convolution fusion | flops 4831838208 | bytes 14942208 | tf_op jit(solution)/shard_map/dot_general | solution.py:39
  499.6 0.0 slice-done.12
  499.6 0.0 slice-done.13
  499.6 0.0 slice-start.8
  499.6 8.7 %fusion.9 = f32[2048,768]{1,0:T(8,128)} fusion(bf16[2048,1536]{1,0:T(8,128)(2,1)S(1)} %bitcast.88, bf16[3,3,1536,768]{3,2,1,0:T(8,128)(2,1)} %param.5), kind=kOutput, calls=%fused_computation.26 | convolution fusion | flops 4831838208 | bytes 14942208 | tf_op jit(solution)/shard_map/dot_general | solution.py:39
  508.4 0.0 slice-start.6
  508.4 9.0 %fusion.5 = f32[2048,768]{1,0:T(8,128)} fusion(bf16[2048,1536]{1,0:T(8,128)(2,1)S(1)} %bitcast.85, bf16[3,3,1536,768]{3,2,1,0:T(8,128)(2,1)} %param.5), kind=kOutput, calls=%fused_computation.22 | convolution fusion | flops 4831838208 | bytes 14942208 | tf_op jit(solution)/shard_map/dot_general | solution.py:39
  517.4 0.0 slice-start.4
  517.4 8.7 %fusion.3 = f32[2048,768]{1,0:T(8,128)} fusion(bf16[2048,1536]{1,0:T(8,128)(2,1)S(1)} %bitcast.82, bf16[3,3,1536,768]{3,2,1,0:T(8,128)(2,1)} %param.5), kind=kOutput, calls=%fused_computation.20 | convolution fusion | flops 4831838208 | bytes 14942208 | tf_op jit(solution)/shard_map/dot_general | solution.py:39
  526.1 0.0 slice-start.2
  526.1 8.7 %fusion.1 = f32[2048,768]{1,0:T(8,128)} fusion(bf16[2048,1536]{1,0:T(8,128)(2,1)S(1)} %bitcast.79, bf16[3,3,1536,768]{3,2,1,0:T(8,128)(2,1)} %param.5), kind=kOutput, calls=%fused_computation.18 | convolution fusion | flops 4831838208 | bytes 14942208 | tf_op jit(solution)/shard_map/dot_general | solution.py:39
  534.8 0.0 slice-done.4
  534.8 0.0 slice-start
  534.8 8.7 %fusion.15 = f32[2048,768]{1,0:T(8,128)} fusion(bf16[2048,1536]{1,0:T(8,128)(2,1)S(1)} %bitcast.76, bf16[3,3,1536,768]{3,2,1,0:T(8,128)(2,1)} %param.5), kind=kOutput, calls=%fused_computation.32 | convolution fusion | flops 4831838208 | bytes 14942208 | tf_op jit(solution)/shard_map/dot_general | solution.py:39
  543.6 8.7 %fusion.7 = f32[2048,768]{1,0:T(8,128)} fusion(bf16[2048,1536]{1,0:T(8,128)(2,1)S(1)} %bitcast.73, bf16[3,3,1536,768]{3,2,1,0:T(8,128)(2,1)} %param.5), kind=kOutput, calls=%fused_computation.24 | convolution fusion | flops 4831838208 | bytes 14942208 | tf_op jit(solution)/shard_map/dot_general | solution.py:39
  552.3 20.2 %add_convert_fusion = bf16[2048,768]{1,0:T(8,128)(2,1)} fusion(f32[2048,768]{1,0:T(8,128)} %fusion.1, f32[2048,768]{1,0:T(8,128)} %fusion.3, f32[2048,768]{1,0:T(8,128)} %fusion.5, f32[2048,768]{1,0:T(8,128)} %fusion.7, f32[2048,768]{1,0:T(8,128)} %fusion.9, f32[2048,768]{1,0:T(8,128)} %fusion.11, f32[2048,768]{1,0:T(8,128)} %fusion.15, ...), kind=kOutput, calls=%fused_computation | convolution fusion | flops 4845993984 | bytes 62128128 | tf_op jit(solution)/shard_map/dot_general | solution.py:39
  572.6 0.0 reduce-scatter.5.cloned.1.call-update
  572.6 36.3 %reduce-scatter.5.cloned.1.call-done = bf16[512,768]{1,0:T(8,128)(2,1)} async-done(((bf16[2048,768]{1,0:T(8,128)(2,1)}), bf16[512,768]{1,0:T(8,128)(2,1)}) %reduce-scatter.5.cloned.1.call-update) | async-done | bytes 786448 | tf_op jit(solution)/shard_map/reduce_scatter | solution.py:42
  608.9 2.2 fusion.26
  (30 shorter events, 0.0 us)
Async XLA Ops:
  6.5 33.6 %all-gather.3.cloned.1.call-start = ((), (), s32[]{:S(2)}) async-start(), calls=%async_computation.2 | async-start | bytes 3932160 | tf_op jit(solution)/shard_map/all_gather | solution.py:8
  7.3 335.7 %reduce-scatter.3.cloned.1.call-start = ((), (), s32[]{:S(2)}) async-start(), calls=%async_computation.3 | async-start | bytes 14155776 | tf_op jit(solution)/shard_map/reduce_scatter | solution.py:21
  61.7 4.0 copy-start.1
  67.5 3.9 copy-start
  135.5 308.5 %all-gather.5.cloned.1.call-start = ((), (), s32[]{:S(2)}) async-start(), calls=%async_computation.4 | async-start | bytes 7077888 | tf_op jit(solution)/shard_map/all_gather | solution.py:28
  345.6 263.2 %reduce-scatter.5.cloned.1.call-start = ((), (), s32[]{:S(2)}) async-start(), calls=%async_computation.5 | async-start | bytes 3932160 | tf_op jit(solution)/shard_map/reduce_scatter | solution.py:42
  481.1 9.7 %copy-start.2 = (bf16[32,64,1536]{2,1,0:T(8,128)(2,1)S(1)}, bf16[32,64,1536]{2,1,0:T(8,128)(2,1)}, u32[]{:S(2)}) copy-start(bf16[32,64,1536]{2,1,0:T(8,128)(2,1)} %get-tuple-element.7) | copy-start | bytes 18874372
  481.1 18.5 %slice-start.12 = ((s8[6291456]{0:T(1024)(128)(4,1)}), s8[4194304]{0:T(1024)(128)(4,1)S(1)}, s32[]{:S(2)}) async-start(s8[6291456]{0:T(1024)(128)(4,1)} %bitcast.86), calls=%async_computation.18 | async-start | bytes 8388608
  490.8 8.8 %slice-start.13 = ((s8[6291456]{0:T(1024)(128)(4,1)}), s8[2097152]{0:T(1024)(128)(4,1)S(1)}, s32[]{:S(2)}) async-start(s8[6291456]{0:T(1024)(128)(4,1)} %bitcast.86), calls=%async_computation.19 | async-start | bytes 4194304
  490.8 17.5 %slice-start.10 = ((s8[6291456]{0:T(1024)(128)(4,1)}), s8[4194304]{0:T(1024)(128)(4,1)S(1)}, s32[]{:S(2)}) async-start(s8[6291456]{0:T(1024)(128)(4,1)} %bitcast.83), calls=%async_computation.16 | async-start | bytes 8388608
  499.6 8.8 %slice-start.11 = ((s8[6291456]{0:T(1024)(128)(4,1)}), s8[2097152]{0:T(1024)(128)(4,1)S(1)}, s32[]{:S(2)}) async-start(s8[6291456]{0:T(1024)(128)(4,1)} %bitcast.83), calls=%async_computation.17 | async-start | bytes 4194304
  499.6 17.8 %slice-start.8 = ((s8[6291456]{0:T(1024)(128)(4,1)}), s8[4194304]{0:T(1024)(128)(4,1)S(1)}, s32[]{:S(2)}) async-start(s8[6291456]{0:T(1024)(128)(4,1)} %bitcast.80), calls=%async_computation.14 | async-start | bytes 8388608
  508.4 9.0 %slice-start.9 = ((s8[6291456]{0:T(1024)(128)(4,1)}), s8[2097152]{0:T(1024)(128)(4,1)S(1)}, s32[]{:S(2)}) async-start(s8[6291456]{0:T(1024)(128)(4,1)} %bitcast.80), calls=%async_computation.15 | async-start | bytes 4194304
  508.4 17.7 %slice-start.6 = ((s8[6291456]{0:T(1024)(128)(4,1)}), s8[4194304]{0:T(1024)(128)(4,1)S(1)}, s32[]{:S(2)}) async-start(s8[6291456]{0:T(1024)(128)(4,1)} %bitcast.77), calls=%async_computation.12 | async-start | bytes 8388608
  517.4 8.7 %slice-start.7 = ((s8[6291456]{0:T(1024)(128)(4,1)}), s8[2097152]{0:T(1024)(128)(4,1)S(1)}, s32[]{:S(2)}) async-start(s8[6291456]{0:T(1024)(128)(4,1)} %bitcast.77), calls=%async_computation.13 | async-start | bytes 4194304
  517.4 17.4 %slice-start.4 = ((s8[6291456]{0:T(1024)(128)(4,1)}), s8[4194304]{0:T(1024)(128)(4,1)S(1)}, s32[]{:S(2)}) async-start(s8[6291456]{0:T(1024)(128)(4,1)} %bitcast.74), calls=%async_computation.10 | async-start | bytes 8388608
  526.1 8.7 %slice-start.5 = ((s8[6291456]{0:T(1024)(128)(4,1)}), s8[2097152]{0:T(1024)(128)(4,1)S(1)}, s32[]{:S(2)}) async-start(s8[6291456]{0:T(1024)(128)(4,1)} %bitcast.74), calls=%async_computation.11 | async-start | bytes 4194304
  526.1 17.5 %slice-start.2 = ((s8[6291456]{0:T(1024)(128)(4,1)}), s8[4194304]{0:T(1024)(128)(4,1)S(1)}, s32[]{:S(2)}) async-start(s8[6291456]{0:T(1024)(128)(4,1)} %bitcast.72), calls=%async_computation.8 | async-start | bytes 8388608
  534.8 8.8 %slice-start.3 = ((s8[6291456]{0:T(1024)(128)(4,1)}), s8[2097152]{0:T(1024)(128)(4,1)S(1)}, s32[]{:S(2)}) async-start(s8[6291456]{0:T(1024)(128)(4,1)} %bitcast.72), calls=%async_computation.9 | async-start | bytes 4194304
  534.8 17.5 %slice-start = ((s8[6291456]{0:T(1024)(128)(4,1)}), s8[4194304]{0:T(1024)(128)(4,1)S(1)}, s32[]{:S(2)}) async-start(s8[6291456]{0:T(1024)(128)(4,1)} %bitcast.59), calls=%async_computation.6 | async-start | bytes 8388608
  543.6 8.7 %slice-start.1 = ((s8[6291456]{0:T(1024)(128)(4,1)}), s8[2097152]{0:T(1024)(128)(4,1)S(1)}, s32[]{:S(2)}) async-start(s8[6291456]{0:T(1024)(128)(4,1)} %bitcast.59), calls=%async_computation.7 | async-start | bytes 4194304
  552.3 56.6 %copy-start.3 = (bf16[8,64,768]{2,1,0:T(8,128)(2,1)S(1)}, bf16[8,64,768]{2,1,0:T(8,128)(2,1)}, u32[]{:S(2)}) copy-start(bf16[8,64,768]{2,1,0:T(8,128)(2,1)} %param.3) | copy-start | bytes 2359300
Sparse Core Ops, SparseCore 0:
  8.9 31.2 all-gather.2
  135.6 207.2 reduce-scatter.2
  345.8 98.1 all-gather.4
  572.7 36.1 reduce-scatter.4
where the time goes:
time: 618 us
  waiting for transfers between devices  376 us (61%)
  matrix products  145 us (23%)
  local copies, waits for them, and re-layouts  78.4 us (13%)
  between operations  13.3 us (2%)
    reduce_scatter x1, waiting for transfers between devices, local(): lax.psum_scatter(jnp.dot(columns, flat_kernel, preferred_element_type=jnp...  207 us
    all_gather x1, waiting for transfers between devices, local(): gathered = lax.all_gather(hidden, ('row', 'slab'), axis=0, tiled=True)  98.2 us
    dot_general x9, matrix products, local(): jnp.dot(window, second_weight[vertical, sideways], preferred_element_type...  91.3 us
    dot_general x1, matrix products, local(): jnp.dot(columns, flat_kernel, preferred_element_type=jnp.float32)  54.1 us
    slice x1, local copies, waits for them, and re-layouts, local(): padded_hidden[vertical:vertical + lines, sideways:sideways + width, :]  37.2 us
    reduce_scatter x1, waiting for transfers between devices, local(): lax.psum_scatter(total.astype(jnp.bfloat16), 'col', scatter_dimension=0,...  36.3 us
    all_gather x1, waiting for transfers between devices, local(): full_input = lax.all_gather(inputs, 'col', axis=0, tiled=True)  32.9 us
    slice x1, local copies, waits for them, and re-layouts, local(): window = padded[vertical:vertical + height, sideways:sideways + width, :]  21.5 us
  transfers between devices with their start and end apart: 4, of which 4 were waited for; matrix products, arithmetic and copies ran while one was open for 0% of the time, Pallas kernels for 0%

commit v1 on v0

v1 whole, which is shorter than its diff:
```python
import functools

import jax
import jax.numpy as jnp
from jax import lax
from jax.experimental import pallas as pl
from jax.experimental.pallas import tpu as pltpu
from jax.sharding import PartitionSpec as P

CHUNKS = 3


def tile_of(size):
    return 256 if size % 256 == 0 else size


def conv_kernel(height, width, with_total, x_ref, w_ref, *rest):
    if with_total:
        total_ref, out_ref, wide = rest
    else:
        out_ref, wide = rest
    depth = x_ref.shape[1]

    @pl.when(pl.program_id(0) == 0)
    def _():
        edge = jnp.zeros((width, 3 * depth), wide.dtype)
        wide[0:width, :] = edge
        wide[(height + 1) * width : (height + 2) * width, :] = edge

        @pl.loop(0, height)
        def _(line):
            start = pl.multiple_of(line * width, width)
            there = pl.multiple_of((line + 1) * width, width)
            block = x_ref[pl.ds(start, width), :]
            long = block.astype(jnp.float32)
            place = lax.broadcasted_iota(jnp.int32, (width, depth), 0)
            before = jnp.where(place == 0, 0.0, pltpu.roll(long, 1, 0))
            after = jnp.where(place == width - 1, 0.0, pltpu.roll(long, width - 1, 0))
            whole = jnp.concatenate([before.astype(wide.dtype), block, after.astype(wide.dtype)], axis=1)
            wide[pl.ds(there, width), :] = whole

    pixels = height * width
    step = 1024

    @pl.loop(0, pixels // step)
    def _(part):
        base = pl.multiple_of(part * step, step)
        sums = None
        for vertical in range(3):
            kernel = w_ref[vertical].reshape(3 * depth, w_ref.shape[3])
            term = jnp.dot(
                wide[pl.ds(pl.multiple_of(base + vertical * width, width), step), :],
                kernel,
                preferred_element_type=jnp.float32,
            )
            sums = term if sums is None else sums + term
        if with_total:
            sums = sums + total_ref[pl.ds(base, step), :]
        out_ref[pl.ds(base, step), :] = sums.astype(out_ref.dtype)


def conv(x, weight, height, width, in_chunk, in_size, out_start, out_size, total, out_dtype):
    pixels = height * width
    tile = tile_of(out_size)
    first_tile = out_start // tile
    in_specs = [
        pl.BlockSpec((pixels, in_size), lambda j: (0, 0), pipeline_mode=pl.Buffered(1)),
        pl.BlockSpec((3, 3, in_size, tile), lambda j: (0, 0, in_chunk, first_tile + j)),
    ]
    args = [x, weight]
    if total is not None:
        in_specs.append(pl.BlockSpec((pixels, tile), lambda j: (0, j)))
        args.append(total)
    return pl.pallas_call(
        functools.partial(conv_kernel, height, width, total is not None),
        grid=(out_size // tile,),
        in_specs=in_specs,
        out_specs=pl.BlockSpec((pixels, tile), lambda j: (0, j)),
        out_shape=jax.ShapeDtypeStruct((pixels, out_size), out_dtype),
        scratch_shapes=[pltpu.VMEM(((height + 2) * width, 3 * in_size), jnp.bfloat16)],
        compiler_params=pltpu.CompilerParams(
            dimension_semantics=("arbitrary",), vmem_limit_bytes=48 * 1024 * 1024
        ),
        cost_estimate=pl.CostEstimate(
            flops=2 * pixels * 9 * in_size * out_size,
            bytes_accessed=2 * (9 * in_size * out_size + pixels * in_size + pixels * out_size),
            transcendentals=0,
        ),
    )(*args)


def local(inputs, first_weight, second_weight):
    full_input = lax.all_gather(inputs, "col", axis=0, tiled=True)
    height, width, depth = full_input.shape
    pixels = height * width
    flat = full_input.reshape(pixels, depth)
    out_first = first_weight.shape[3]
    out_second = second_weight.shape[3]
    size = out_first // CHUNKS
    hiddens = []
    for chunk in range(CHUNKS):
        first = conv(flat, first_weight, height, width, 0, depth, chunk * size, size, None, jnp.bfloat16)
        first = lax.psum_scatter(first, ("row", "slab"), scatter_dimension=0, tiled=True)
        hidden = jax.nn.silu(first.astype(jnp.float32)).astype(jnp.bfloat16)
        hiddens.append(lax.all_gather(hidden, ("row", "slab"), axis=0, tiled=True))
    total = None
    for chunk in range(CHUNKS):
        last = chunk == CHUNKS - 1
        total = conv(
            hiddens[chunk], second_weight, height, width, chunk, size, 0, out_second, total,
            jnp.bfloat16 if last else jnp.float32,
        )
    second = lax.psum_scatter(total, "col", scatter_dimension=0, tiled=True).astype(jnp.float32)
    combined = inputs.astype(jnp.float32) + second.reshape(inputs.shape)
    return combined.astype(jnp.bfloat16)


def solution(mesh):
    in_specs = (
        P("col", None, ("row", "slab")),
        P(None, None, ("row", "slab"), "col"),
        P(None, None, "col", ("row", "slab")),
    )
    out_specs = P("col", None, ("row", "slab"))
    return jax.shard_map(local, mesh=mesh, in_specs=in_specs, out_specs=out_specs, check_vma=False)
```

time: 618 us -> 488 us (0.79)
  matrix products: 145 us -> 0 us
  Pallas kernels: 0 us -> 120 us
  local copies, waits for them, and re-layouts: 78.4 us -> 6.67 us
  waiting for transfers between devices: 376 us -> 339 us
    dot_general x10 -> x0, matrix products: 145 us -> none  [the longest x9 91.3 us: local(): jnp.dot(window, second_weight[vertical, sideways], preferred_element_type...]
    pallas_call x0 -> x6, Pallas kernels: none -> 120 us  [conv(): pl.pallas_call(functools.partial(conv_kernel, height, width, total is not...]
    slice x2 -> x0, local copies, waits for them, and re-layouts: 58.7 us -> none  [the longest x1 37.2 us: local(): padded_hidden[vertical:vertical + lines, sideways:sideways + width, :]]
    reduce_scatter x2 -> x4, waiting for transfers between devices: 244 us -> 201 us  [the longest x3 165 us: local(): lax.psum_scatter(first, ('row', 'slab'), scatter_dimension=0, tiled=True)]
    unnamed x44 -> x12, local copies, waits for them, and re-layouts: 17.8 us -> 6.67 us
    all_gather x1 -> x3, waiting for transfers between devices: 98.2 us -> 105 us  [local(): hiddens.append(lax.all_gather(hidden, ('row', 'slab'), axis=0, tiled=True))]
  transfers between devices with their start and end apart: 4 -> 8, of which waited for: 4 -> 8; matrix products, arithmetic and copies ran while one was open for 0% -> 1% of each run, Pallas kernels for 0% -> 16%
where the time goes in v1:
time: 488 us
  waiting for transfers between devices  339 us (69%)
  Pallas kernels  120 us (25%)
  between operations  13.5 us (3%)
  other arithmetic  7.63 us (2%)
  local copies, waits for them, and re-layouts  6.67 us (1%)
    reduce_scatter x3, waiting for transfers between devices, local(): lax.psum_scatter(first, ('row', 'slab'), scatter_dimension=0, tiled=True)  165 us
    pallas_call x6, Pallas kernels, conv(): pl.pallas_call(functools.partial(conv_kernel, height, width, total is not...  120 us
    all_gather x3, waiting for transfers between devices, local(): hiddens.append(lax.all_gather(hidden, ('row', 'slab'), axis=0, tiled=True))  105 us
    reduce_scatter x1, waiting for transfers between devices, local(): lax.psum_scatter(total, 'col', scatter_dimension=0, tiled=True)  36.6 us
    all_gather x1, waiting for transfers between devices, local(): full_input = lax.all_gather(inputs, 'col', axis=0, tiled=True)  32.9 us
  transfers between devices with their start and end apart: 8, of which 8 were waited for; matrix products, arithmetic and copies ran while one was open for 1% of the time, Pallas kernels for 16%

profile of v1, /device:TPU:0, one launch (start us, length us, event | category | flops | bytes accessed | tf_op | source)
XLA Modules:
  0.0 487.6 jit_solution(96111694711498384)
XLA Ops:
  6.5 0.0 all-gather.5.cloned.1.call-start
  6.5 0.7 all-gather.5.cloned.1.call-update
  7.3 0.0 reduce-scatter.9.cloned.1.call-start
  7.3 32.9 %all-gather.5.cloned.1.call-done = bf16[32,64,768]{2,1,0:T(8,128)(2,1)} async-done(((bf16[8,64,768]{2,1,0:T(8,128)(2,1)}), bf16[32,64,768]{2,1,0:T(8,128)(2,1)}) %all-gather.5.cloned.1.call-update) | async-done | bytes 3145744 | tf_op jit(solution)/shard_map/all_gather | solution.py:93
  40.2 0.0 copy-start
  40.2 1.9 copy-done
  42.1 0.0 copy-start.1
  42.1 20.0 %shard_map.39 = bf16[2048,512]{1,0:T(8,128)(2,1)} custom-call(bf16[2048,768]{1,0:T(8,128)(2,1)S(1)} %bitcast.3, bf16[3,3,768,1536]{3,2,1,0:T(8,128)(2,1)} %w_ref.8), custom_call_target="tpu_custom_call" | custom-call | flops 14495514624 | bytes 12320768 | tf_op jit(solution)/shard_map/pallas_call | solution.py:74
  62.0 0.0 reduce-scatter.9.cloned.1.call-update
  62.1 0.0 reduce-scatter.7.cloned.1.call-start
  62.1 0.0 copy-done.1
  62.1 19.8 %shard_map.38 = bf16[2048,512]{1,0:T(8,128)(2,1)} custom-call(bf16[2048,768]{1,0:T(8,128)(2,1)S(1)} %bitcast.4, bf16[3,3,768,1536]{3,2,1,0:T(8,128)(2,1)} %w_ref.8), custom_call_target="tpu_custom_call" | custom-call | flops 14495514624 | bytes 12320768 | tf_op jit(solution)/shard_map/pallas_call | solution.py:74
  81.9 0.0 reduce-scatter.7.cloned.1.call-update
  82.0 0.0 reduce-scatter.5.cloned.1.call-start
  82.0 19.9 %shard_map.37 = bf16[2048,512]{1,0:T(8,128)(2,1)} custom-call(bf16[2048,768]{1,0:T(8,128)(2,1)S(1)} %bitcast.5, bf16[3,3,768,1536]{3,2,1,0:T(8,128)(2,1)} %w_ref.8), custom_call_target="tpu_custom_call" | custom-call | flops 14495514624 | bytes 12320768 | tf_op jit(solution)/shard_map/pallas_call | solution.py:74
  101.9 0.0 reduce-scatter.5.cloned.1.call-update
  101.9 0.0 all-gather.11.cloned.1.call-start
  102.0 27.9 %reduce-scatter.9.cloned.1.call-done = bf16[256,512]{1,0:T(8,128)(2,1)} async-done(((bf16[2048,512]{1,0:T(8,128)(2,1)}), bf16[256,512]{1,0:T(8,128)(2,1)}) %reduce-scatter.9.cloned.1.call-update) | async-done | bytes 262160 | tf_op jit(solution)/shard_map/reduce_scatter | solution.py:103
  129.9 1.8 fusion.12
  131.8 0.0 all-gather.11.cloned.1.call-update
  131.8 0.0 all-gather.9.cloned.1.call-start
  131.8 68.4 %reduce-scatter.7.cloned.1.call-done = bf16[256,512]{1,0:T(8,128)(2,1)} async-done(((bf16[2048,512]{1,0:T(8,128)(2,1)}), bf16[256,512]{1,0:T(8,128)(2,1)}) %reduce-scatter.7.cloned.1.call-update) | async-done | bytes 262160 | tf_op jit(solution)/shard_map/reduce_scatter | solution.py:103
  200.2 1.8 fusion.8
  202.0 0.0 all-gather.9.cloned.1.call-update
  202.0 0.0 all-gather.7.cloned.1.call-start
  202.1 68.2 %reduce-scatter.5.cloned.1.call-done = bf16[256,512]{1,0:T(8,128)(2,1)} async-done(((bf16[2048,512]{1,0:T(8,128)(2,1)}), bf16[256,512]{1,0:T(8,128)(2,1)}) %reduce-scatter.5.cloned.1.call-update) | async-done | bytes 262160 | tf_op jit(solution)/shard_map/reduce_scatter | solution.py:103
  270.3 1.8 fusion.4
  272.1 0.0 all-gather.7.cloned.1.call-update
  272.1 0.2 reduce-scatter.11.cloned.1.call-start
  272.4 48.2 %all-gather.11.cloned.1.call-done.x_ref = bf16[2048,512]{1,0:T(8,128)(2,1)} async-done(((bf16[256,512]{1,0:T(8,128)(2,1)}), bf16[2048,512]{1,0:T(8,128)(2,1)}) %all-gather.11.cloned.1.call-update) | async-done | bytes 2097168 | tf_op jit(solution)/shard_map/all_gather | solution.py:105
  320.5 0.0 copy-start.2
  320.6 1.6 copy-done.2
  322.1 19.8 %shard_map.40.rest_0_ = f32[2048,768]{1,0:T(8,128)} custom-call(bf16[2048,512]{1,0:T(8,128)(2,1)S(1)} %copy-done.2, bf16[3,3,1536,768]{3,2,1,0:T(8,128)(2,1)} %w_ref.11), custom_call_target="tpu_custom_call" | custom-call | flops 14495514624 | bytes 12320768 | tf_op jit(solution)/shard_map/pallas_call | solution.py:74
  342.0 28.4 %all-gather.9.cloned.1.call-done.x_ref = bf16[2048,512]{1,0:T(8,128)(2,1)} async-done(((bf16[256,512]{1,0:T(8,128)(2,1)}), bf16[2048,512]{1,0:T(8,128)(2,1)}) %all-gather.9.cloned.1.call-update) | async-done | bytes 2097168 | tf_op jit(solution)/shard_map/all_gather | solution.py:105
  370.3 0.0 copy-start.3
  370.3 1.6 copy-done.3
  371.9 20.4 %shard_map.41.rest_0_ = f32[2048,768]{1,0:T(8,128)} custom-call(bf16[2048,512]{1,0:T(8,128)(2,1)S(1)} %copy-done.3, bf16[3,3,1536,768]{3,2,1,0:T(8,128)(2,1)} %w_ref.11, f32[2048,768]{1,0:T(8,128)} %shard_map.40.rest_0_), custom_call_target="tpu_custom_call" | custom-call | flops 14495514624 | bytes 12320768 | tf_op jit(solution)/shard_map/pallas_call | solution.py:74
  392.3 28.0 %all-gather.7.cloned.1.call-done.x_ref = bf16[2048,512]{1,0:T(8,128)(2,1)} async-done(((bf16[256,512]{1,0:T(8,128)(2,1)}), bf16[2048,512]{1,0:T(8,128)(2,1)}) %all-gather.7.cloned.1.call-update) | async-done | bytes 2097168 | tf_op jit(solution)/shard_map/all_gather | solution.py:105
  420.3 0.0 copy-start.4
  420.3 1.6 copy-done.4
  421.9 20.0 %shard_map.42 = bf16[2048,768]{1,0:T(8,128)(2,1)} custom-call(bf16[2048,512]{1,0:T(8,128)(2,1)S(1)} %copy-done.4, bf16[3,3,1536,768]{3,2,1,0:T(8,128)(2,1)} %w_ref.11, f32[2048,768]{1,0:T(8,128)} %shard_map.41.rest_0_), custom_call_target="tpu_custom_call" | custom-call | flops 14495514624 | bytes 12320768 | tf_op jit(solution)/shard_map/pallas_call | solution.py:74
  441.9 0.0 copy-start.5
  441.9 0.0 reduce-scatter.11.cloned.1.call-update
  441.9 36.6 %reduce-scatter.11.cloned.1.call-done = bf16[512,768]{1,0:T(8,128)(2,1)} async-done(((bf16[2048,768]{1,0:T(8,128)(2,1)}), bf16[512,768]{1,0:T(8,128)(2,1)}) %reduce-scatter.11.cloned.1.call-update) | async-done | bytes 786448 | tf_op jit(solution)/shard_map/reduce_scatter | solution.py:113
  478.5 0.0 copy-done.5
  478.5 2.2 fusion
Async XLA Ops:
  6.5 33.6 %all-gather.5.cloned.1.call-start = ((), (), s32[]{:S(2)}) async-start(), calls=%async_computation.4 | async-start | bytes 3932160 | tf_op jit(solution)/shard_map/all_gather | solution.py:93
  7.3 122.7 %reduce-scatter.9.cloned.1.call-start = ((), (), s32[]{:S(2)}) async-start(), calls=%async_computation.9 | async-start | bytes 2359296 | tf_op jit(solution)/shard_map/reduce_scatter | solution.py:103
  40.2 1.9 copy-start
  42.1 20.1 %copy-start.1 = (bf16[32,64,768]{2,1,0:T(8,128)(2,1)S(1)}, bf16[32,64,768]{2,1,0:T(8,128)(2,1)}, u32[]{:S(2)}) copy-start(bf16[32,64,768]{2,1,0:T(8,128)(2,1)} %all-gather.5.cloned.1.call-done) | copy-start | bytes 9437188
  62.1 138.1 %reduce-scatter.7.cloned.1.call-start = ((), (), s32[]{:S(2)}) async-start(), calls=%async_computation.7 | async-start | bytes 2359296 | tf_op jit(solution)/shard_map/reduce_scatter | solution.py:103
  82.0 188.3 %reduce-scatter.5.cloned.1.call-start = ((), (), s32[]{:S(2)}) async-start(), calls=%async_computation.5 | async-start | bytes 2359296 | tf_op jit(solution)/shard_map/reduce_scatter | solution.py:103
  101.9 218.6 %all-gather.11.cloned.1.call-start = ((), (), s32[]{:S(2)}) async-start(), calls=%async_computation.10 | async-start | bytes 2359296 | tf_op jit(solution)/shard_map/all_gather | solution.py:105
  131.8 238.5 %all-gather.9.cloned.1.call-start = ((), (), s32[]{:S(2)}) async-start(), calls=%async_computation.8 | async-start | bytes 2359296 | tf_op jit(solution)/shard_map/all_gather | solution.py:105
  202.0 218.3 %all-gather.7.cloned.1.call-start = ((), (), s32[]{:S(2)}) async-start(), calls=%async_computation.6 | async-start | bytes 2359296 | tf_op jit(solution)/shard_map/all_gather | solution.py:105
  272.1 206.4 %reduce-scatter.11.cloned.1.call-start = ((), (), s32[]{:S(2)}) async-start(), calls=%async_computation.11 | async-start | bytes 3932160 | tf_op jit(solution)/shard_map/reduce_scatter | solution.py:113
  320.5 1.6 copy-start.2
  370.3 1.6 copy-start.3
  420.3 1.6 copy-start.4
  441.9 36.6 %copy-start.5 = (bf16[8,64,768]{2,1,0:T(8,128)(2,1)S(1)}, bf16[8,64,768]{2,1,0:T(8,128)(2,1)}, u32[]{:S(2)}) copy-start(bf16[8,64,768]{2,1,0:T(8,128)(2,1)} %param.3) | copy-start | bytes 2359300
Sparse Core Ops, SparseCore 0:
  8.9 31.2 all-gather.4
  62.2 67.6 reduce-scatter.8
  133.5 66.6 reduce-scatter.6
  203.6 66.6 reduce-scatter.4
  272.3 48.2 all-gather.10
  322.5 47.7 all-gather.8
  372.5 47.7 all-gather.6
  442.0 36.4 reduce-scatter.10

commit v2 on v1

--- a/solution.py
+++ b/solution.py
@@ -89,20 +89,176 @@
     )(*args)
 
 
+def shift(x, axis, sources, by):
+    return lax.ppermute(x, axis, [(i, i + by) for i in sources])
+
+
+def wide(value):
+    return value.astype(jnp.float32)
+
+
+def piece(pieces, index):
+    n = pieces.shape[0]
+    return lax.dynamic_index_in_dim(pieces, jnp.clip(index, 0, n - 1), 0, keepdims=False)
+
+
+def cut(x, n):
+    return x.reshape((n, x.shape[0] // n) + x.shape[1:])
+
+
+def line_sends(pieces, axis, step):
+    n, me = pieces.shape[0], lax.axis_index(axis)
+    return piece(pieces, me + n - step), piece(pieces, me - n + step)
+
+
+def line_move(sends, axis, step):
+    n = lax.axis_size(axis)
+    up = shift(sends[0], axis, range(0, step), 1)
+    return up, shift(sends[1], axis, range(n - step, n), -1)
+
+
+def line_finish(pieces, got, axis):
+    n, me = pieces.shape[0], lax.axis_index(axis)
+    for step in range(2, n):
+        sends = [
+            (wide(mine) + wide(came)).astype(pieces.dtype)
+            for mine, came in zip(line_sends(pieces, axis, step), got)
+        ]
+        got = line_move(sends, axis, step)
+    return wide(piece(pieces, me)) + wide(got[0]) + wide(got[1])
+
+
+def scatter_sum(x, axis):
+    n = lax.axis_size(axis)
+    if n > 4 or n < 3:
+        return lax.psum_scatter(x, axis, scatter_dimension=0, tiled=True)
+    pieces = cut(x, n)
+    got = line_move(line_sends(pieces, axis, 1), axis, 1)
+    return line_finish(pieces, got, axis).astype(x.dtype)
+
+
+def gather(x, axis):
+    n = lax.axis_size(axis)
+    me = lax.axis_index(axis)
+    if n > 4:
+        return lax.all_gather(x, axis, axis=0, tiled=True)
+    if n == 2:
+        other = lax.ppermute(x, axis, [(0, 1), (1, 0)])
+        line = [other, x, other]
+    else:
+        line = [x]
+        up = down = x
+        for step in range(1, n):
+            up = shift(up, axis, range(step - 1, n - 1), 1)
+            down = shift(down, axis, range(1, n - step + 1), -1)
+            line = [up] + line + [down]
+    size = x.shape[0]
+    return lax.dynamic_slice_in_dim(jnp.concatenate(line, axis=0), (n - 1 - me) * size, n * size, 0)
+
+
+def flip(x, axis, bit):
+    return lax.ppermute(x, axis, [(i, i ^ bit) for i in range(lax.axis_size(axis))])
+
+
+def gather_col(x):
+    if lax.axis_size("col") != 4:
+        return lax.all_gather(x, "col", axis=0, tiled=True)
+    me = lax.axis_index("col")
+    core, far = me % 2, me // 2
+    beside = flip(x, "col", 1)
+    across = flip(x, "col", 2)
+    corner = flip(across, "col", 1)
+
+    def pair(mine, other):
+        return jnp.where(core == 0, jnp.stack([mine, other]), jnp.stack([other, mine]))
+
+    near, away = pair(x, beside), pair(across, corner)
+    both = jnp.where(far == 0, jnp.stack([near, away]), jnp.stack([away, near]))
+    return both.reshape((4 * x.shape[0],) + x.shape[1:])
+
+
+def scatter_col(x):
+    if lax.axis_size("col") != 4:
+        return lax.psum_scatter(x, "col", scatter_dimension=0, tiled=True).astype(jnp.float32)
+    me = lax.axis_index("col")
+    core, far = me % 2, me // 2
+    rows = x.shape[0] // 4
+    pieces = x.reshape((2, 2, rows) + x.shape[1:])
+
+    def pick(array, index, axis):
+        return lax.dynamic_index_in_dim(array, index, axis, keepdims=False)
+
+    other = flip(pick(pieces, 1 - core, 1), "col", 1)
+    halves = (pick(pieces, core, 1).astype(jnp.float32) + other.astype(jnp.float32))
+    sent = pick(halves, 1 - far, 0).astype(x.dtype)
+    return pick(halves, far, 0) + flip(sent, "col", 2).astype(jnp.float32)
+
+
+def finish(first):
+    hidden = jax.nn.silu(first.astype(jnp.float32)).astype(jnp.bfloat16)
+    return gather(hidden, "slab")
+
+
+def after(values, *earlier):
+    tied = lax.optimization_barrier((*values, *earlier))
+    return tied[: len(values)]
+
+
+def hidden_chunks(layer_one):
+    if lax.axis_size("row") != 2 or lax.axis_size("slab") != 4:
+        return [
+            gather(finish(scatter_sum(scatter_sum(layer_one(chunk, ()), "row"), "slab")), "row")
+            for chunk in range(CHUNKS)
+        ]
+    row = lax.axis_index("row")
+
+    def halves(first):
+        pieces = cut(first, 2)
+        return piece(pieces, row), piece(pieces, 1 - row)
+
+    def exchange(sent):
+        return lax.ppermute(sent, "row", [(0, 1), (1, 0)])
+
+    def added(kept, other):
+        return cut((wide(kept) + wide(other)).astype(kept.dtype), 4)
+
+    kept0, sent0 = halves(layer_one(0, ()))
+    other0 = exchange(sent0)
+    kept1, sent1 = halves(layer_one(1, (sent0,)))
+    other1 = exchange(sent1)
+    sum0 = added(kept0, other0)
+    sends0 = line_sends(sum0, "slab", 1)
+    got0 = line_move(sends0, "slab", 1)
+    kept2, sent2 = halves(layer_one(2, (sent1, *sends0)))
+    other2 = exchange(sent2)
+    up0, down0, other1 = after((*got0, other1), sent2)
+    sum1 = added(kept1, other1)
+    sends1 = line_sends(sum1, "slab", 1)
+    got1 = line_move(sends1, "slab", 1)
+    first0 = line_finish(sum0, (up0, down0), "slab")
+    parts0 = finish(first0)
+    parts1 = finish(line_finish(sum1, got1, "slab"))
+    (other2,) = after((other2,), parts0)
+    sum2 = added(kept2, other2)
+    got2 = line_move(line_sends(sum2, "slab", 1), "slab", 1)
+    parts2 = finish(line_finish(sum2, got2, "slab"))
+    return [gather(part, "row") for part in (parts0, parts1, parts2)]
+
+
 def local(inputs, first_weight, second_weight):
-    full_input = lax.all_gather(inputs, "col", axis=0, tiled=True)
+    full_input = gather_col(inputs)
     height, width, depth = full_input.shape
     pixels = height * width
     flat = full_input.reshape(pixels, depth)
     out_first = first_weight.shape[3]
     out_second = second_weight.shape[3]
     size = out_first // CHUNKS
-    hiddens = []
-    for chunk in range(CHUNKS):
-        first = conv(flat, first_weight, height, width, 0, depth, chunk * size, size, None, jnp.bfloat16)
-        first = lax.psum_scatter(first, ("row", "slab"), scatter_dimension=0, tiled=True)
-        hidden = jax.nn.silu(first.astype(jnp.float32)).astype(jnp.bfloat16)
-        hiddens.append(lax.all_gather(hidden, ("row", "slab"), axis=0, tiled=True))
+
+    def layer_one(chunk, earlier):
+        (source,) = after((flat,), *earlier) if earlier else (flat,)
+        return conv(source, first_weight, height, width, 0, depth, chunk * size, size, None, jnp.bfloat16)
+
+    hiddens = hidden_chunks(layer_one)
     total = None
     for chunk in range(CHUNKS):
         last = chunk == CHUNKS - 1
@@ -110,7 +266,7 @@
             hiddens[chunk], second_weight, height, width, chunk, size, 0, out_second, total,
             jnp.bfloat16 if last else jnp.float32,
         )
-    second = lax.psum_scatter(total, "col", scatter_dimension=0, tiled=True).astype(jnp.float32)
+    second = scatter_col(total)
     combined = inputs.astype(jnp.float32) + second.reshape(inputs.shape)
     return combined.astype(jnp.bfloat16)
 

time: 488 us -> 340 us (0.70)
  waiting for transfers between devices: 339 us -> 78.2 us
  starting transfers between devices: 0.47 us -> 90.5 us
  other arithmetic: 7.63 us -> 35.7 us
  between operations: 13.5 us -> 0.7 us
  local copies, waits for them, and re-layouts: 6.67 us -> 16.9 us
    reduce_scatter x4 -> x0, waiting for transfers between devices: 201 us -> none  [the longest x3 165 us: local(): lax.psum_scatter(first, ('row', 'slab'), scatter_dimension=0, tiled=True)]
    all_gather x4 -> x0, waiting for transfers between devices: 137 us -> none  [the longest x3 105 us: local(): hiddens.append(lax.all_gather(hidden, ('row', 'slab'), axis=0, tiled=True))]
    ppermute x0 -> x47, starting transfers between devices: none -> 90.5 us  [the longest x36 78.5 us: shift(): return lax.ppermute(x, axis, [(i, i + by) for i in sources])]
    ppermute x0 -> x47, waiting for transfers between devices: none -> 78.2 us  [the longest x5 40.2 us: flip(): lax.ppermute(x, axis, [(i, i ^ bit) for i in range(lax.axis_size(axis))])]
    concatenate x0 -> x3, other arithmetic: none -> 13.7 us  [gather(): jnp.concatenate(line, axis=0)]
    convert_element_type x3 -> x15, other arithmetic: 5.44 us -> 15.3 us  [the longest x9 11.5 us: line_finish(): (wide(mine) + wide(came)).astype(pieces.dtype)]
    unnamed x12 -> x32, local copies, waits for them, and re-layouts: 6.67 us -> 11.5 us
  transfers between devices with their start and end apart: 8 -> 47, of which waited for: 8 -> 16; matrix products, arithmetic and copies ran while one was open for 1% -> 12% of each run, Pallas kernels for 16% -> 23%
where the time goes in v2:
time: 340 us; the launch traced here: 338 us
  Pallas kernels  116 us (34%)
  starting transfers between devices  90.5 us (27%)
  waiting for transfers between devices  78.2 us (23%)
  other arithmetic  35.7 us (11%)
  local copies, waits for them, and re-layouts  16.9 us (5%)
    pallas_call x6, Pallas kernels, conv(): pl.pallas_call(functools.partial(conv_kernel, height, width, total is not...  116 us
    ppermute x36, starting transfers between devices, shift(): return lax.ppermute(x, axis, [(i, i + by) for i in sources])  78.5 us
    ppermute x5, waiting for transfers between devices, flip(): lax.ppermute(x, axis, [(i, i ^ bit) for i in range(lax.axis_size(axis))])  40.2 us
    ppermute x36, waiting for transfers between devices, shift(): return lax.ppermute(x, axis, [(i, i + by) for i in sources])  30 us
    concatenate x3, other arithmetic, gather(): jnp.concatenate(line, axis=0)  13.7 us
    unnamed x32, local copies, waits for them, and re-layouts  11.5 us
    convert_element_type x9, other arithmetic, line_finish(): (wide(mine) + wide(came)).astype(pieces.dtype)  11.5 us
    ppermute x3, waiting for transfers between devices, exchange(): return lax.ppermute(sent, 'row', [(0, 1), (1, 0)])  7.97 us
  transfers between devices with their start and end apart: 47, of which 16 were waited for; matrix products, arithmetic and copies ran while one was open for 12% of the time, Pallas kernels for 23%

profile of v2, /device:TPU:0, one launch (start us, length us, event | category | flops | bytes accessed | tf_op | source)
XLA Modules:
  0.0 338.2 jit_solution(5028061822848724379)
XLA Ops:
  0.0 3.0 collective-permute-start.1
  3.0 17.7 %collective-permute-done.1 = bf16[8,64,768]{2,1,0:T(8,128)(2,1)S(1)} collective-permute-done((bf16[8,64,768]{2,1,0:T(8,128)(2,1)}, bf16[8,64,768]{2,1,0:T(8,128)(2,1)S(1)}, u32[]{:S(2)}, u32[]{:S(2)}) %collective-permute-start.1) | collective-permute-done | bytes 786464 | tf_op jit(solution)/shard_map/ppermute | solution.py:160
  20.7 1.6 maximum_select_fusion.1
  23.8 19.0 %shard_map.37 = bf16[2048,512]{1,0:T(8,128)(2,1)S(1)} custom-call(bf16[2048,768]{1,0:T(8,128)(2,1)S(1)} %bitcast.94, bf16[3,3,768,1536]{3,2,1,0:T(8,128)(2,1)} %w_ref.8), custom_call_target="tpu_custom_call" | custom-call | flops 14495514624 | bytes 12320768 | tf_op jit(solution)/shard_map/pallas_call | solution.py:74
  42.9 1.8 collective-permute-start.3
  44.6 19.0 %shard_map.38 = bf16[2048,512]{1,0:T(8,128)(2,1)S(1)} custom-call(bf16[2048,768]{1,0:T(8,128)(2,1)S(1)} %bitcast.95, bf16[3,3,768,1536]{3,2,1,0:T(8,128)(2,1)} %w_ref.8), custom_call_target="tpu_custom_call" | custom-call | flops 14495514624 | bytes 12320768 | tf_op jit(solution)/shard_map/pallas_call | solution.py:74
  64.1 4.9 %collective-permute-done.3 = bf16[1024,512]{1,0:T(8,128)(2,1)S(1)} collective-permute-done((bf16[1024,512]{1,0:T(8,128)(2,1)S(1)}, bf16[1024,512]{1,0:T(8,128)(2,1)S(1)}, u32[]{:S(2)}, u32[]{:S(2)}) %collective-permute-start.3) | collective-permute-done | bytes 1048608 | tf_op jit(solution)/shard_map/ppermute | solution.py:220
  69.3 3.7 %collective-permute-start.5 = (bf16[256,512]{1,0:T(8,128)(2,1)S(1)}, bf16[256,512]{1,0:T(8,128)(2,1)S(1)}, u32[]{:S(2)}, u32[]{:S(2)}) collective-permute-start(bf16[256,512]{1,0:T(8,128)(2,1)S(1)} %get-tuple-element.28), channel_id=1, source_target_pairs={{0,1},{4,5},{8,9},{12,13},{16,17},{20,21},{24,25},{28,29}} | collective-permute-start | bytes 786440 | tf_op jit(solution)/shard_map/ppermute | solution.py:93
  73.7 19.0 %shard_map.39 = bf16[2048,512]{1,0:T(8,128)(2,1)S(1)} custom-call(bf16[2048,768]{1,0:T(8,128)(2,1)S(1)} %bitcast.96, bf16[3,3,768,1536]{3,2,1,0:T(8,128)(2,1)} %w_ref.8), custom_call_target="tpu_custom_call" | custom-call | flops 14495514624 | bytes 12320768 | tf_op jit(solution)/shard_map/pallas_call | solution.py:74
  94.6 2.0 collective-permute-start.8
  97.6 3.5 %collective-permute-start.31 = (bf16[256,512]{1,0:T(8,128)(2,1)}, bf16[256,512]{1,0:T(8,128)(2,1)}, u32[]{:S(2)}, u32[]{:S(2)}) collective-permute-start(bf16[256,512]{1,0:T(8,128)(2,1)} %get-tuple-element.19), channel_id=1, source_target_pairs={{0,1},{4,5},{8,9},{12,13},{16,17},{20,21},{24,25},{28,29}} | collective-permute-start | bytes 786440 | tf_op jit(solution)/shard_map/ppermute | solution.py:93
  101.8 2.1 fusion.23
  106.6 1.7 fusion.12
  108.3 5.0 %collective-permute-start.32 = (bf16[256,512]{1,0:T(8,128)(2,1)}, bf16[256,512]{1,0:T(8,128)(2,1)}, u32[]{:S(2)}, u32[]{:S(2)}) collective-permute-start(bf16[256,512]{1,0:T(8,128)(2,1)} %fusion.12), channel_id=1, source_target_pairs={{0,1},{1,2},{4,5},{5,6},{8,9},{9,10},{12,13},{13,14},{16,17},{17,1... | collective-permute-start | bytes 786440 | tf_op jit(solution)/shard_map/ppermute | solution.py:93
  113.4 4.5 %collective-permute-start.9 = (bf16[256,512]{1,0:T(8,128)(2,1)}, bf16[256,512]{1,0:T(8,128)(2,1)}, u32[]{:S(2)}, u32[]{:S(2)}) collective-permute-start(bf16[256,512]{1,0:T(8,128)(2,1)} %get-tuple-element.25), channel_id=1, source_target_pairs={{0,1},{1,2},{2,3},{4,5},{5,6},{6,7},{8,9},{9,10},{10,11},{12,13},{... | collective-permute-start | bytes 786440 | tf_op jit(solution)/shard_map/ppermute | solution.py:93
  117.9 1.8 fusion.21
  121.0 2.0 fusion.13
  124.3 4.5 %collective-permute-start.33 = (bf16[256,512]{1,0:T(8,128)(2,1)}, bf16[256,512]{1,0:T(8,128)(2,1)S(1)}, u32[]{:S(2)}, u32[]{:S(2)}) collective-permute-start(bf16[256,512]{1,0:T(8,128)(2,1)} %get-tuple-element.17), channel_id=1, source_target_pairs={{0,1},{1,2},{2,3},{4,5},{5,6},{6,7},{8,9},{9,10},{10,11},{12,13},{... | collective-permute-start | bytes 786440 | tf_op jit(solution)/shard_map/ppermute | solution.py:93
  130.2 4.6 %collective-permute-start.12 = (bf16[256,512]{1,0:T(8,128)(2,1)S(1)}, bf16[256,512]{1,0:T(8,128)(2,1)S(1)}, u32[]{:S(2)}, u32[]{:S(2)}) collective-permute-start(bf16[256,512]{1,0:T(8,128)(2,1)S(1)} %multiply_convert_fusion.2), channel_id=1, source_target_pairs={{0,1},{1,2},{2,3},{4,5},{5,6},{6,7},{8,9},{9,10},{10,11},{12,13},{... | collective-permute-start | bytes 786440 | tf_op jit(solution)/shard_map/ppermute | solution.py:93
  140.0 3.3 collective-permute-done.15
  144.6 4.0 %collective-permute-done.36 = bf16[256,512]{1,0:T(8,128)(2,1)S(1)} collective-permute-done((bf16[256,512]{1,0:T(8,128)(2,1)S(1)}, bf16[256,512]{1,0:T(8,128)(2,1)S(1)}, u32[]{:S(2)}, u32[]{:S(2)}) %collective-permute-start.36) | collective-permute-done | bytes 262176 | tf_op jit(solution)/shard_map/ppermute | solution.py:93
  148.8 4.1 %collective-permute-start.37 = (bf16[256,512]{1,0:T(8,128)(2,1)S(1)}, bf16[256,512]{1,0:T(8,128)(2,1)}, u32[]{:S(2)}, u32[]{:S(2)}) collective-permute-start(bf16[256,512]{1,0:T(8,128)(2,1)S(1)} %multiply_convert_fusion), channel_id=1, source_target_pairs={{0,1},{1,2},{2,3},{4,5},{5,6},{6,7},{8,9},{9,10},{10,11},{12,13},{... | collective-permute-start | bytes 786440 | tf_op jit(solution)/shard_map/ppermute | solution.py:93
  153.6 1.6 collective-permute-start.4
  164.2 2.0 collective-permute-done.17
  167.3 3.1 collective-permute-done.4
  170.4 1.5 fusion.7
  172.7 3.7 %collective-permute-start.18 = (bf16[256,512]{1,0:T(8,128)(2,1)S(1)}, bf16[256,512]{1,0:T(8,128)(2,1)S(1)}, u32[]{:S(2)}, u32[]{:S(2)}) collective-permute-start(bf16[256,512]{1,0:T(8,128)(2,1)S(1)} %get-tuple-element.23), channel_id=1, source_target_pairs={{0,1},{4,5},{8,9},{12,13},{16,17},{20,21},{24,25},{28,29}} | collective-permute-start | bytes 786440 | tf_op jit(solution)/shard_map/ppermute | solution.py:93
  180.4 2.5 collective-permute-done.18
  183.7 5.1 %collective-permute-start.19 = (bf16[256,512]{1,0:T(8,128)(2,1)}, bf16[256,512]{1,0:T(8,128)(2,1)}, u32[]{:S(2)}, u32[]{:S(2)}) collective-permute-start(bf16[256,512]{1,0:T(8,128)(2,1)} %fusion.17), channel_id=1, source_target_pairs={{0,1},{1,2},{4,5},{5,6},{8,9},{9,10},{12,13},{13,14},{16,17},{17,1... | collective-permute-start | bytes 786440 | tf_op jit(solution)/shard_map/ppermute | solution.py:93
  197.4 5.2 %collective-permute-start.20 = (bf16[256,512]{1,0:T(8,128)(2,1)S(1)}, bf16[256,512]{1,0:T(8,128)(2,1)S(1)}, u32[]{:S(2)}, u32[]{:S(2)}) collective-permute-start(bf16[256,512]{1,0:T(8,128)(2,1)S(1)} %get-tuple-element.21), channel_id=1, source_target_pairs={{0,1},{1,2},{2,3},{4,5},{5,6},{6,7},{8,9},{9,10},{10,11},{12,13},{... | collective-permute-start | bytes 786440 | tf_op jit(solution)/shard_map/ppermute | solution.py:93
  205.7 3.1 collective-permute-done.20
  208.7 3.3 collective-permute-done.23
  212.2 3.9 %collective-permute-start.24 = (bf16[256,512]{1,0:T(8,128)(2,1)S(1)}, bf16[256,512]{1,0:T(8,128)(2,1)S(1)}, u32[]{:S(2)}, u32[]{:S(2)}) collective-permute-start(bf16[256,512]{1,0:T(8,128)(2,1)S(1)} %multiply_convert_fusion.1), channel_id=1, source_target_pairs={{0,1},{1,2},{2,3},{4,5},{5,6},{6,7},{8,9},{9,10},{10,11},{12,13},{... | collective-permute-start | bytes 786440 | tf_op jit(solution)/shard_map/ppermute | solution.py:93
  216.1 4.6 %fusion.1.x_ref = bf16[2048,512]{1,0:T(8,128)(2,1)S(1)} fusion(s32[]{:T(128)S(6)} %select_n.114, bf16[1024,512]{1,0:T(8,128)(2,1)S(1)} %collective-permute-done.44, bf16[1024,512]{1,0:T(8,128)(2,1)S(1)} %copy-done.2), kind=kLoop, calls=%fused_computation.12 | loop fusion | flops 6291456 | bytes 4194308 | tf_op jit(solution)/shard_map/concatenate | solution.py:156
  222.7 19.7 %shard_map.40.rest_0_ = f32[2048,768]{1,0:T(8,128)} custom-call(bf16[2048,512]{1,0:T(8,128)(2,1)S(1)} %fusion.1.x_ref, bf16[3,3,1536,768]{3,2,1,0:T(8,128)(2,1)} %w_ref.11), custom_call_target="tpu_custom_call" | custom-call | flops 14495514624 | bytes 12320768 | tf_op jit(solution)/shard_map/pallas_call | solution.py:74
  244.7 4.6 %fusion.3.x_ref = bf16[2048,512]{1,0:T(8,128)(2,1)S(1)} fusion(s32[]{:T(128)S(6)} %select_n.114, bf16[1024,512]{1,0:T(8,128)(2,1)S(1)} %collective-permute-done.43, bf16[1024,512]{1,0:T(8,128)(2,1)S(1)} %constant_dynamic-slice_fusion), kind=kLoop, calls=%fused_computation.14 | loop fusion | flops 6291456 | bytes 4194308 | tf_op jit(solution)/shard_map/concatenate | solution.py:156
  249.3 4.1 %collective-permute-done.28 = bf16[256,512]{1,0:T(8,128)(2,1)S(1)} collective-permute-done((bf16[256,512]{1,0:T(8,128)(2,1)S(1)}, bf16[256,512]{1,0:T(8,128)(2,1)S(1)}, u32[]{:S(2)}, u32[]{:S(2)}) %collective-permute-start.28) | collective-permute-done | bytes 262176 | tf_op jit(solution)/shard_map/ppermute | solution.py:93
  254.8 6.8 %collective-permute-done.29 = bf16[256,512]{1,0:T(8,128)(2,1)S(1)} collective-permute-done((bf16[256,512]{1,0:T(8,128)(2,1)S(1)}, bf16[256,512]{1,0:T(8,128)(2,1)S(1)}, u32[]{:S(2)}, u32[]{:S(2)}) %collective-permute-start.29) | collective-permute-done | bytes 262176 | tf_op jit(solution)/shard_map/ppermute | solution.py:93
  261.7 1.6 collective-permute-start.30
  263.3 20.3 %shard_map.41.rest_0_ = f32[2048,768]{1,0:T(8,128)} custom-call(bf16[2048,512]{1,0:T(8,128)(2,1)S(1)} %fusion.3.x_ref, bf16[3,3,1536,768]{3,2,1,0:T(8,128)(2,1)} %w_ref.11, f32[2048,768]{1,0:T(8,128)} %shard_map.40.rest_0_), custom_call_target="tpu_custom_call" | custom-call | flops 14495514624 | bytes 12320768 | tf_op jit(solution)/shard_map/pallas_call | solution.py:74
  283.6 4.6 %fusion.5.x_ref = bf16[2048,512]{1,0:T(8,128)(2,1)S(1)} fusion(s32[]{:T(128)S(6)} %select_n.114, bf16[1024,512]{1,0:T(8,128)(2,1)S(1)} %collective-permute-done.30, bf16[1024,512]{1,0:T(8,128)(2,1)S(1)} %constant_dynamic-slice_fusion.1), kind=kLoop, calls=%fused_computation.16 | loop fusion | flops 6291456 | bytes 4194308 | tf_op jit(solution)/shard_map/concatenate | solution.py:156
  288.2 19.2 %shard_map.42 = bf16[2048,768]{1,0:T(8,128)(2,1)S(1)} custom-call(bf16[2048,512]{1,0:T(8,128)(2,1)S(1)} %fusion.5.x_ref, bf16[3,3,1536,768]{3,2,1,0:T(8,128)(2,1)} %w_ref.11, f32[2048,768]{1,0:T(8,128)} %shard_map.41.rest_0_), custom_call_target="tpu_custom_call" | custom-call | flops 14495514624 | bytes 12320768 | tf_op jit(solution)/shard_map/pallas_call | solution.py:74
  308.7 3.7 %collective-permute-done.45 = bf16[2,512,768]{2,1,0:T(8,128)(2,1)} collective-permute-done((bf16[2,512,768]{2,1,0:T(8,128)(2,1)}, bf16[2,512,768]{2,1,0:T(8,128)(2,1)}, u32[]{:S(2)}, u32[]{:S(2)}) %collective-permute-start.45) | collective-permute-done | bytes 1572896 | tf_op jit(solution)/shard_map/ppermute | solution.py:160
  312.5 1.7 convert_add_fusion
  314.2 1.6 copy-done
  315.9 1.6 collective-permute-start.46
  317.5 18.1 %collective-permute-done.46 = bf16[512,768]{1,0:T(8,128)(2,1)S(1)} collective-permute-done((bf16[512,768]{1,0:T(8,128)(2,1)S(1)}, bf16[512,768]{1,0:T(8,128)(2,1)S(1)}, u32[]{:S(2)}, u32[]{:S(2)}) %collective-permute-start.46) | collective-permute-done | bytes 786464 | tf_op jit(solution)/shard_map/ppermute | solution.py:160
  335.5 1.6 bitcast_add_fusion
  (122 shorter events, 56.1 us)
Async XLA Ops:
  0.0 20.7 %collective-permute-start.1 = (bf16[8,64,768]{2,1,0:T(8,128)(2,1)}, bf16[8,64,768]{2,1,0:T(8,128)(2,1)S(1)}, u32[]{:S(2)}, u32[]{:S(2)}) collective-permute-start(bf16[8,64,768]{2,1,0:T(8,128)(2,1)} %param.3), channel_id=1, source_target_pairs={{0,8},{4,12},{8,0},{12,4},{1,9},{5,13},{9,1},{13,5},{2,10},{6,14},... | collective-permute-start | bytes 2359304 | tf_op jit(solution)/shard_map/ppermute | solution.py:160
  3.0 17.8 %collective-permute-start = (bf16[8,64,768]{2,1,0:T(8,128)(2,1)}, bf16[8,64,768]{2,1,0:T(8,128)(2,1)S(1)}, u32[]{:S(2)}, u32[]{:S(2)}) collective-permute-start(bf16[8,64,768]{2,1,0:T(8,128)(2,1)} %param.3), channel_id=1, source_target_pairs={{0,4},{4,0},{8,12},{12,8},{1,5},{5,1},{9,13},{13,9},{2,6},{6,2},{1... | collective-permute-start | bytes 2359304 | tf_op jit(solution)/shard_map/ppermute | solution.py:160
  20.7 2.3 collective-permute-start.2
  42.9 26.1 %collective-permute-start.3 = (bf16[1024,512]{1,0:T(8,128)(2,1)S(1)}, bf16[1024,512]{1,0:T(8,128)(2,1)S(1)}, u32[]{:S(2)}, u32[]{:S(2)}) collective-permute-start(bf16[1024,512]{1,0:T(8,128)(2,1)S(1)} %dynamic-slice_bitcast_fusion.3), channel_id=1, source_target_pairs={{0,16},{16,0},{1,17},{17,1},{2,18},{18,2},{3,19},{19,3},{4,20},{20... | collective-permute-start | bytes 3145736 | tf_op jit(solution)/shard_map/ppermute | solution.py:220
  63.7 30.1 %collective-permute-start.7 = (bf16[1024,512]{1,0:T(8,128)(2,1)S(1)}, bf16[1024,512]{1,0:T(8,128)(2,1)S(1)}, u32[]{:S(2)}, u32[]{:S(2)}) collective-permute-start(bf16[1024,512]{1,0:T(8,128)(2,1)S(1)} %dynamic-slice_bitcast_fusion.2), channel_id=1, source_target_pairs={{0,16},{16,0},{1,17},{17,1},{2,18},{18,2},{3,19},{19,3},{4,20},{20... | collective-permute-start | bytes 3145736 | tf_op jit(solution)/shard_map/ppermute | solution.py:220
  69.2 24.6 %copy-start.1 = (bf16[1024,512]{1,0:T(8,128)(2,1)}, bf16[1024,512]{1,0:T(8,128)(2,1)S(1)}, u32[]{:S(2)}) copy-start(bf16[1024,512]{1,0:T(8,128)(2,1)S(1)} %fusion.8) | copy-start | bytes 3145732
  69.3 24.5 %collective-permute-start.5 = (bf16[256,512]{1,0:T(8,128)(2,1)S(1)}, bf16[256,512]{1,0:T(8,128)(2,1)S(1)}, u32[]{:S(2)}, u32[]{:S(2)}) collective-permute-start(bf16[256,512]{1,0:T(8,128)(2,1)S(1)} %get-tuple-element.28), channel_id=1, source_target_pairs={{0,1},{4,5},{8,9},{12,13},{16,17},{20,21},{24,25},{28,29}} | collective-permute-start | bytes 786440 | tf_op jit(solution)/shard_map/ppermute | solution.py:93
  73.0 20.8 %collective-permute-start.6 = (bf16[256,512]{1,0:T(8,128)(2,1)S(1)}, bf16[256,512]{1,0:T(8,128)(2,1)S(1)}, u32[]{:S(2)}, u32[]{:S(2)}) collective-permute-start(bf16[256,512]{1,0:T(8,128)(2,1)S(1)} %get-tuple-element.27), channel_id=1, source_target_pairs={{3,2},{7,6},{11,10},{15,14},{19,18},{23,22},{27,26},{31,30}} | collective-permute-start | bytes 786440 | tf_op jit(solution)/shard_map/ppermute | solution.py:93
  94.6 7.1 %collective-permute-start.8 = (bf16[256,512]{1,0:T(8,128)(2,1)}, bf16[256,512]{1,0:T(8,128)(2,1)}, u32[]{:S(2)}, u32[]{:S(2)}) collective-permute-start(bf16[256,512]{1,0:T(8,128)(2,1)} %fusion.22), channel_id=1, source_target_pairs={{0,1},{1,2},{4,5},{5,6},{8,9},{9,10},{12,13},{13,14},{16,17},{17,1... | collective-permute-start | bytes 786440 | tf_op jit(solution)/shard_map/ppermute | solution.py:93
  97.6 9.0 %collective-permute-start.31 = (bf16[256,512]{1,0:T(8,128)(2,1)}, bf16[256,512]{1,0:T(8,128)(2,1)}, u32[]{:S(2)}, u32[]{:S(2)}) collective-permute-start(bf16[256,512]{1,0:T(8,128)(2,1)} %get-tuple-element.19), channel_id=1, source_target_pairs={{0,1},{4,5},{8,9},{12,13},{16,17},{20,21},{24,25},{28,29}} | collective-permute-start | bytes 786440 | tf_op jit(solution)/shard_map/ppermute | solution.py:93
  103.9 14.0 %collective-permute-start.10 = (bf16[256,512]{1,0:T(8,128)(2,1)}, bf16[256,512]{1,0:T(8,128)(2,1)}, u32[]{:S(2)}, u32[]{:S(2)}) collective-permute-start(bf16[256,512]{1,0:T(8,128)(2,1)} %get-tuple-element.26), channel_id=1, source_target_pairs={{2,1},{3,2},{6,5},{7,6},{10,9},{11,10},{14,13},{15,14},{18,17},{19... | collective-permute-start | bytes 786440 | tf_op jit(solution)/shard_map/ppermute | solution.py:93
  105.3 15.7 %collective-permute-start.34 = (bf16[256,512]{1,0:T(8,128)(2,1)S(1)}, bf16[256,512]{1,0:T(8,128)(2,1)}, u32[]{:S(2)}, u32[]{:S(2)}) collective-permute-start(bf16[256,512]{1,0:T(8,128)(2,1)S(1)} %get-tuple-element.20), channel_id=1, source_target_pairs={{3,2},{7,6},{11,10},{15,14},{19,18},{23,22},{27,26},{31,30}} | collective-permute-start | bytes 786440 | tf_op jit(solution)/shard_map/ppermute | solution.py:93
  108.3 12.7 %collective-permute-start.32 = (bf16[256,512]{1,0:T(8,128)(2,1)}, bf16[256,512]{1,0:T(8,128)(2,1)}, u32[]{:S(2)}, u32[]{:S(2)}) collective-permute-start(bf16[256,512]{1,0:T(8,128)(2,1)} %fusion.12), channel_id=1, source_target_pairs={{0,1},{1,2},{4,5},{5,6},{8,9},{9,10},{12,13},{13,14},{16,17},{17,1... | collective-permute-start | bytes 786440 | tf_op jit(solution)/shard_map/ppermute | solution.py:93
  113.4 15.5 %collective-permute-start.9 = (bf16[256,512]{1,0:T(8,128)(2,1)}, bf16[256,512]{1,0:T(8,128)(2,1)}, u32[]{:S(2)}, u32[]{:S(2)}) collective-permute-start(bf16[256,512]{1,0:T(8,128)(2,1)} %get-tuple-element.25), channel_id=1, source_target_pairs={{0,1},{1,2},{2,3},{4,5},{5,6},{6,7},{8,9},{9,10},{10,11},{12,13},{... | collective-permute-start | bytes 786440 | tf_op jit(solution)/shard_map/ppermute | solution.py:93
  119.7 9.2 %collective-permute-start.11 = (bf16[256,512]{1,0:T(8,128)(2,1)}, bf16[256,512]{1,0:T(8,128)(2,1)}, u32[]{:S(2)}, u32[]{:S(2)}) collective-permute-start(bf16[256,512]{1,0:T(8,128)(2,1)} %fusion.21), channel_id=1, source_target_pairs={{1,0},{2,1},{3,2},{5,4},{6,5},{7,6},{9,8},{10,9},{11,10},{13,12},{... | collective-permute-start | bytes 786440 | tf_op jit(solution)/shard_map/ppermute | solution.py:93
  123.0 13.1 %collective-permute-start.35 = (bf16[256,512]{1,0:T(8,128)(2,1)}, bf16[256,512]{1,0:T(8,128)(2,1)}, u32[]{:S(2)}, u32[]{:S(2)}) collective-permute-start(bf16[256,512]{1,0:T(8,128)(2,1)} %get-tuple-element.18), channel_id=1, source_target_pairs={{2,1},{3,2},{6,5},{7,6},{10,9},{11,10},{14,13},{15,14},{18,17},{19... | collective-permute-start | bytes 786440 | tf_op jit(solution)/shard_map/ppermute | solution.py:93
  124.3 20.2 %collective-permute-start.33 = (bf16[256,512]{1,0:T(8,128)(2,1)}, bf16[256,512]{1,0:T(8,128)(2,1)S(1)}, u32[]{:S(2)}, u32[]{:S(2)}) collective-permute-start(bf16[256,512]{1,0:T(8,128)(2,1)} %get-tuple-element.17), channel_id=1, source_target_pairs={{0,1},{1,2},{2,3},{4,5},{5,6},{6,7},{8,9},{9,10},{10,11},{12,13},{... | collective-permute-start | bytes 786440 | tf_op jit(solution)/shard_map/ppermute | solution.py:93
  130.2 8.4 %collective-permute-start.12 = (bf16[256,512]{1,0:T(8,128)(2,1)S(1)}, bf16[256,512]{1,0:T(8,128)(2,1)S(1)}, u32[]{:S(2)}, u32[]{:S(2)}) collective-permute-start(bf16[256,512]{1,0:T(8,128)(2,1)S(1)} %multiply_convert_fusion.2), channel_id=1, source_target_pairs={{0,1},{1,2},{2,3},{4,5},{5,6},{6,7},{8,9},{9,10},{10,11},{12,13},{... | collective-permute-start | bytes 786440 | tf_op jit(solution)/shard_map/ppermute | solution.py:93
  134.7 8.5 %collective-permute-start.15 = (bf16[256,512]{1,0:T(8,128)(2,1)S(1)}, bf16[256,512]{1,0:T(8,128)(2,1)}, u32[]{:S(2)}, u32[]{:S(2)}) collective-permute-start(bf16[256,512]{1,0:T(8,128)(2,1)S(1)} %multiply_convert_fusion.2), channel_id=1, source_target_pairs={{1,0},{2,1},{3,2},{5,4},{6,5},{7,6},{9,8},{10,9},{11,10},{13,12},{... | collective-permute-start | bytes 786440 | tf_op jit(solution)/shard_map/ppermute | solution.py:93
  137.1 11.6 %collective-permute-start.36 = (bf16[256,512]{1,0:T(8,128)(2,1)S(1)}, bf16[256,512]{1,0:T(8,128)(2,1)S(1)}, u32[]{:S(2)}, u32[]{:S(2)}) collective-permute-start(bf16[256,512]{1,0:T(8,128)(2,1)S(1)} %fusion.11), channel_id=1, source_target_pairs={{1,0},{2,1},{3,2},{5,4},{6,5},{7,6},{9,8},{10,9},{11,10},{13,12},{... | collective-permute-start | bytes 786440 | tf_op jit(solution)/shard_map/ppermute | solution.py:93
  138.6 14.3 %collective-permute-start.13 = (bf16[256,512]{1,0:T(8,128)(2,1)S(1)}, bf16[256,512]{1,0:T(8,128)(2,1)}, u32[]{:S(2)}, u32[]{:S(2)}) collective-permute-start(bf16[256,512]{1,0:T(8,128)(2,1)S(1)} %collective-permute-done.12), channel_id=1, source_target_pairs={{1,2},{2,3},{5,6},{6,7},{9,10},{10,11},{13,14},{14,15},{17,18},{18... | collective-permute-start | bytes 786440 | tf_op jit(solution)/shard_map/ppermute | solution.py:93
  143.3 13.2 %collective-permute-start.16 = (bf16[256,512]{1,0:T(8,128)(2,1)}, bf16[256,512]{1,0:T(8,128)(2,1)}, u32[]{:S(2)}, u32[]{:S(2)}) collective-permute-start(bf16[256,512]{1,0:T(8,128)(2,1)} %collective-permute-done.15), channel_id=1, source_target_pairs={{1,0},{2,1},{5,4},{6,5},{9,8},{10,9},{13,12},{14,13},{17,16},{18,1... | collective-permute-start | bytes 786440 | tf_op jit(solution)/shard_map/ppermute | solution.py:93
  148.8 9.1 %collective-permute-start.37 = (bf16[256,512]{1,0:T(8,128)(2,1)S(1)}, bf16[256,512]{1,0:T(8,128)(2,1)}, u32[]{:S(2)}, u32[]{:S(2)}) collective-permute-start(bf16[256,512]{1,0:T(8,128)(2,1)S(1)} %multiply_convert_fusion), channel_id=1, source_target_pairs={{0,1},{1,2},{2,3},{4,5},{5,6},{6,7},{8,9},{9,10},{10,11},{12,13},{... | collective-permute-start | bytes 786440 | tf_op jit(solution)/shard_map/ppermute | solution.py:93
  152.9 6.4 %collective-permute-start.14 = (bf16[256,512]{1,0:T(8,128)(2,1)}, bf16[256,512]{1,0:T(8,128)(2,1)S(1)}, u32[]{:S(2)}, u32[]{:S(2)}) collective-permute-start(bf16[256,512]{1,0:T(8,128)(2,1)} %collective-permute-done.13), channel_id=1, source_target_pairs={{2,3},{6,7},{10,11},{14,15},{18,19},{22,23},{26,27},{30,31}} | collective-permute-start | bytes 786440 | tf_op jit(solution)/shard_map/ppermute | solution.py:93
  153.6 16.8 %collective-permute-start.4 = (bf16[1024,512]{1,0:T(8,128)(2,1)}, bf16[1024,512]{1,0:T(8,128)(2,1)}, u32[]{:S(2)}, u32[]{:S(2)}) collective-permute-start(bf16[1024,512]{1,0:T(8,128)(2,1)} %dynamic-slice_bitcast_fusion.1), channel_id=1, source_target_pairs={{0,16},{16,0},{1,17},{17,1},{2,18},{18,2},{3,19},{19,3},{4,20},{20... | collective-permute-start | bytes 3145736 | tf_op jit(solution)/shard_map/ppermute | solution.py:220
  155.2 21.2 %collective-permute-start.40 = (bf16[256,512]{1,0:T(8,128)(2,1)S(1)}, bf16[256,512]{1,0:T(8,128)(2,1)}, u32[]{:S(2)}, u32[]{:S(2)}) collective-permute-start(bf16[256,512]{1,0:T(8,128)(2,1)S(1)} %multiply_convert_fusion), channel_id=1, source_target_pairs={{1,0},{2,1},{3,2},{5,4},{6,5},{7,6},{9,8},{10,9},{11,10},{13,12},{... | collective-permute-start | bytes 786440 | tf_op jit(solution)/shard_map/ppermute | solution.py:93
  156.5 9.8 %collective-permute-start.17 = (bf16[256,512]{1,0:T(8,128)(2,1)}, bf16[256,512]{1,0:T(8,128)(2,1)S(1)}, u32[]{:S(2)}, u32[]{:S(2)}) collective-permute-start(bf16[256,512]{1,0:T(8,128)(2,1)} %collective-permute-done.16), channel_id=1, source_target_pairs={{1,0},{5,4},{9,8},{13,12},{17,16},{21,20},{25,24},{29,28}} | collective-permute-start | bytes 786440 | tf_op jit(solution)/shard_map/ppermute | solution.py:93
  158.0 21.1 %collective-permute-start.38 = (bf16[256,512]{1,0:T(8,128)(2,1)}, bf16[256,512]{1,0:T(8,128)(2,1)}, u32[]{:S(2)}, u32[]{:S(2)}) collective-permute-start(bf16[256,512]{1,0:T(8,128)(2,1)} %collective-permute-done.37), channel_id=1, source_target_pairs={{1,2},{2,3},{5,6},{6,7},{9,10},{10,11},{13,14},{14,15},{17,18},{18... | collective-permute-start | bytes 786440 | tf_op jit(solution)/shard_map/ppermute | solution.py:93
  172.7 10.2 %collective-permute-start.18 = (bf16[256,512]{1,0:T(8,128)(2,1)S(1)}, bf16[256,512]{1,0:T(8,128)(2,1)S(1)}, u32[]{:S(2)}, u32[]{:S(2)}) collective-permute-start(bf16[256,512]{1,0:T(8,128)(2,1)S(1)} %get-tuple-element.23), channel_id=1, source_target_pairs={{0,1},{4,5},{8,9},{12,13},{16,17},{20,21},{24,25},{28,29}} | collective-permute-start | bytes 786440 | tf_op jit(solution)/shard_map/ppermute | solution.py:93
  176.4 13.9 %collective-permute-start.41 = (bf16[256,512]{1,0:T(8,128)(2,1)}, bf16[256,512]{1,0:T(8,128)(2,1)}, u32[]{:S(2)}, u32[]{:S(2)}) collective-permute-start(bf16[256,512]{1,0:T(8,128)(2,1)} %collective-permute-done.40), channel_id=1, source_target_pairs={{1,0},{2,1},{5,4},{6,5},{9,8},{10,9},{13,12},{14,13},{17,16},{18,1... | collective-permute-start | bytes 786440 | tf_op jit(solution)/shard_map/ppermute | solution.py:93
  177.7 15.9 %collective-permute-start.21 = (bf16[256,512]{1,0:T(8,128)(2,1)}, bf16[256,512]{1,0:T(8,128)(2,1)}, u32[]{:S(2)}, u32[]{:S(2)}) collective-permute-start(bf16[256,512]{1,0:T(8,128)(2,1)} %get-tuple-element.24), channel_id=1, source_target_pairs={{3,2},{7,6},{11,10},{15,14},{19,18},{23,22},{27,26},{31,30}} | collective-permute-start | bytes 786440 | tf_op jit(solution)/shard_map/ppermute | solution.py:93
  179.1 12.5 %collective-permute-start.39 = (bf16[256,512]{1,0:T(8,128)(2,1)}, bf16[256,512]{1,0:T(8,128)(2,1)}, u32[]{:S(2)}, u32[]{:S(2)}) collective-permute-start(bf16[256,512]{1,0:T(8,128)(2,1)} %collective-permute-done.38), channel_id=1, source_target_pairs={{2,3},{6,7},{10,11},{14,15},{18,19},{22,23},{26,27},{30,31}} | collective-permute-start | bytes 786440 | tf_op jit(solution)/shard_map/ppermute | solution.py:93
  183.7 9.8 %collective-permute-start.19 = (bf16[256,512]{1,0:T(8,128)(2,1)}, bf16[256,512]{1,0:T(8,128)(2,1)}, u32[]{:S(2)}, u32[]{:S(2)}) collective-permute-start(bf16[256,512]{1,0:T(8,128)(2,1)} %fusion.17), channel_id=1, source_target_pairs={{0,1},{1,2},{4,5},{5,6},{8,9},{9,10},{12,13},{13,14},{16,17},{17,1... | collective-permute-start | bytes 786440 | tf_op jit(solution)/shard_map/ppermute | solution.py:93
  188.8 27.3 %collective-permute-start.44 = (bf16[1024,512]{1,0:T(8,128)(2,1)S(1)}, bf16[1024,512]{1,0:T(8,128)(2,1)S(1)}, u32[]{:S(2)}, u32[]{:S(2)}) collective-permute-start(bf16[1024,512]{1,0:T(8,128)(2,1)S(1)} %copy-done.2), channel_id=1, source_target_pairs={{0,16},{16,0},{1,17},{17,1},{2,18},{18,2},{3,19},{19,3},{4,20},{20... | collective-permute-start | bytes 3145736 | tf_op jit(solution)/shard_map/ppermute | solution.py:146
  190.3 14.7 %collective-permute-start.42 = (bf16[256,512]{1,0:T(8,128)(2,1)}, bf16[256,512]{1,0:T(8,128)(2,1)S(1)}, u32[]{:S(2)}, u32[]{:S(2)}) collective-permute-start(bf16[256,512]{1,0:T(8,128)(2,1)} %collective-permute-done.41), channel_id=1, source_target_pairs={{1,0},{5,4},{9,8},{13,12},{17,16},{21,20},{25,24},{29,28}} | collective-permute-start | bytes 786440 | tf_op jit(solution)/shard_map/ppermute | solution.py:93
  194.7 7.9 %collective-permute-start.22 = (bf16[256,512]{1,0:T(8,128)(2,1)S(1)}, bf16[256,512]{1,0:T(8,128)(2,1)S(1)}, u32[]{:S(2)}, u32[]{:S(2)}) collective-permute-start(bf16[256,512]{1,0:T(8,128)(2,1)S(1)} %get-tuple-element.22), channel_id=1, source_target_pairs={{2,1},{3,2},{6,5},{7,6},{10,9},{11,10},{14,13},{15,14},{18,17},{19... | collective-permute-start | bytes 786440 | tf_op jit(solution)/shard_map/ppermute | solution.py:93
  197.4 11.3 %collective-permute-start.20 = (bf16[256,512]{1,0:T(8,128)(2,1)S(1)}, bf16[256,512]{1,0:T(8,128)(2,1)S(1)}, u32[]{:S(2)}, u32[]{:S(2)}) collective-permute-start(bf16[256,512]{1,0:T(8,128)(2,1)S(1)} %get-tuple-element.21), channel_id=1, source_target_pairs={{0,1},{1,2},{2,3},{4,5},{5,6},{6,7},{8,9},{9,10},{10,11},{12,13},{... | collective-permute-start | bytes 786440 | tf_op jit(solution)/shard_map/ppermute | solution.py:93
  202.7 9.3 %collective-permute-start.23 = (bf16[256,512]{1,0:T(8,128)(2,1)S(1)}, bf16[256,512]{1,0:T(8,128)(2,1)S(1)}, u32[]{:S(2)}, u32[]{:S(2)}) collective-permute-start(bf16[256,512]{1,0:T(8,128)(2,1)S(1)} %fusion.16), channel_id=1, source_target_pairs={{1,0},{2,1},{3,2},{5,4},{6,5},{7,6},{9,8},{10,9},{11,10},{13,12},{... | collective-permute-start | bytes 786440 | tf_op jit(solution)/shard_map/ppermute | solution.py:93
  205.1 39.6 %collective-permute-start.43 = (bf16[1024,512]{1,0:T(8,128)(2,1)S(1)}, bf16[1024,512]{1,0:T(8,128)(2,1)S(1)}, u32[]{:S(2)}, u32[]{:S(2)}) collective-permute-start(bf16[1024,512]{1,0:T(8,128)(2,1)S(1)} %constant_dynamic-slice_fusion), channel_id=1, source_target_pairs={{0,16},{16,0},{1,17},{17,1},{2,18},{18,2},{3,19},{19,3},{4,20},{20... | collective-permute-start | bytes 3145736 | tf_op jit(solution)/shard_map/ppermute | solution.py:146
  212.2 9.8 %collective-permute-start.24 = (bf16[256,512]{1,0:T(8,128)(2,1)S(1)}, bf16[256,512]{1,0:T(8,128)(2,1)S(1)}, u32[]{:S(2)}, u32[]{:S(2)}) collective-permute-start(bf16[256,512]{1,0:T(8,128)(2,1)S(1)} %multiply_convert_fusion.1), channel_id=1, source_target_pairs={{0,1},{1,2},{2,3},{4,5},{5,6},{6,7},{8,9},{9,10},{10,11},{12,13},{... | collective-permute-start | bytes 786440 | tf_op jit(solution)/shard_map/ppermute | solution.py:93
  220.7 21.7 %collective-permute-start.27 = (bf16[256,512]{1,0:T(8,128)(2,1)S(1)}, bf16[256,512]{1,0:T(8,128)(2,1)S(1)}, u32[]{:S(2)}, u32[]{:S(2)}) collective-permute-start(bf16[256,512]{1,0:T(8,128)(2,1)S(1)} %multiply_convert_fusion.1), channel_id=1, source_target_pairs={{1,0},{2,1},{3,2},{5,4},{6,5},{7,6},{9,8},{10,9},{11,10},{13,12},{... | collective-permute-start | bytes 786440 | tf_op jit(solution)/shard_map/ppermute | solution.py:93
  222.0 21.7 %collective-permute-start.25 = (bf16[256,512]{1,0:T(8,128)(2,1)S(1)}, bf16[256,512]{1,0:T(8,128)(2,1)S(1)}, u32[]{:S(2)}, u32[]{:S(2)}) collective-permute-start(bf16[256,512]{1,0:T(8,128)(2,1)S(1)} %collective-permute-done.24), channel_id=1, source_target_pairs={{1,2},{2,3},{5,6},{6,7},{9,10},{10,11},{13,14},{14,15},{17,18},{18... | collective-permute-start | bytes 786440 | tf_op jit(solution)/shard_map/ppermute | solution.py:93
  242.5 10.9 %collective-permute-start.28 = (bf16[256,512]{1,0:T(8,128)(2,1)S(1)}, bf16[256,512]{1,0:T(8,128)(2,1)S(1)}, u32[]{:S(2)}, u32[]{:S(2)}) collective-permute-start(bf16[256,512]{1,0:T(8,128)(2,1)S(1)} %collective-permute-done.27), channel_id=1, source_target_pairs={{1,0},{2,1},{5,4},{6,5},{9,8},{10,9},{13,12},{14,13},{17,16},{18,1... | collective-permute-start | bytes 786440 | tf_op jit(solution)/shard_map/ppermute | solution.py:93
  243.8 10.9 %collective-permute-start.26 = (bf16[256,512]{1,0:T(8,128)(2,1)S(1)}, bf16[256,512]{1,0:T(8,128)(2,1)S(1)}, u32[]{:S(2)}, u32[]{:S(2)}) collective-permute-start(bf16[256,512]{1,0:T(8,128)(2,1)S(1)} %collective-permute-done.25), channel_id=1, source_target_pairs={{2,3},{6,7},{10,11},{14,15},{18,19},{22,23},{26,27},{30,31}} | collective-permute-start | bytes 786440 | tf_op jit(solution)/shard_map/ppermute | solution.py:93
  253.3 8.3 %collective-permute-start.29 = (bf16[256,512]{1,0:T(8,128)(2,1)S(1)}, bf16[256,512]{1,0:T(8,128)(2,1)S(1)}, u32[]{:S(2)}, u32[]{:S(2)}) collective-permute-start(bf16[256,512]{1,0:T(8,128)(2,1)S(1)} %collective-permute-done.28), channel_id=1, source_target_pairs={{1,0},{5,4},{9,8},{13,12},{17,16},{21,20},{25,24},{29,28}} | collective-permute-start | bytes 786440 | tf_op jit(solution)/shard_map/ppermute | solution.py:93
  261.7 21.9 %collective-permute-start.30 = (bf16[1024,512]{1,0:T(8,128)(2,1)S(1)}, bf16[1024,512]{1,0:T(8,128)(2,1)S(1)}, u32[]{:S(2)}, u32[]{:S(2)}) collective-permute-start(bf16[1024,512]{1,0:T(8,128)(2,1)S(1)} %constant_dynamic-slice_fusion.1), channel_id=1, source_target_pairs={{0,16},{16,0},{1,17},{17,1},{2,18},{18,2},{3,19},{19,3},{4,20},{20... | collective-permute-start | bytes 3145736 | tf_op jit(solution)/shard_map/ppermute | solution.py:146
  308.7 3.8 %collective-permute-start.45 = (bf16[2,512,768]{2,1,0:T(8,128)(2,1)}, bf16[2,512,768]{2,1,0:T(8,128)(2,1)}, u32[]{:S(2)}, u32[]{:S(2)}) collective-permute-start(bf16[2,512,768]{2,1,0:T(8,128)(2,1)} %dynamic-slice_bitcast_fusion), channel_id=1, source_target_pairs={{0,4},{4,0},{8,12},{12,8},{1,5},{5,1},{9,13},{13,9},{2,6},{6,2},{1... | collective-permute-start | bytes 4718600 | tf_op jit(solution)/shard_map/ppermute | solution.py:160
  315.9 19.6 %collective-permute-start.46 = (bf16[512,768]{1,0:T(8,128)(2,1)S(1)}, bf16[512,768]{1,0:T(8,128)(2,1)S(1)}, u32[]{:S(2)}, u32[]{:S(2)}) collective-permute-start(bf16[512,768]{1,0:T(8,128)(2,1)S(1)} %fusion.9), channel_id=1, source_target_pairs={{0,8},{4,12},{8,0},{12,4},{1,9},{5,13},{9,1},{13,5},{2,10},{6,14},... | collective-permute-start | bytes 2359304 | tf_op jit(solution)/shard_map/ppermute | solution.py:160
  (6 other events, 65.8 us)

commit v3 on v1

--- a/solution.py
+++ b/solution.py
@@ -69,7 +69,7 @@
     ]
     args = [x, weight]
     if total is not None:
-        in_specs.append(pl.BlockSpec((pixels, tile), lambda j: (0, j)))
+        in_specs.append(pl.BlockSpec((pixels, tile), lambda j: (0, first_tile + j)))
         args.append(total)
     return pl.pallas_call(
         functools.partial(conv_kernel, height, width, total is not None),
@@ -89,30 +89,148 @@
     )(*args)
 
 
+def wide(value):
+    return value.astype(jnp.float32)
+
+
+def piece(pieces, index, axis=0):
+    return lax.dynamic_index_in_dim(pieces, index, axis, keepdims=False)
+
+
+def cut(x, n):
+    return x.reshape((n, x.shape[0] // n) + x.shape[1:])
+
+
+def flip(x, axis, bit):
+    return lax.ppermute(x, axis, [(i, i ^ bit) for i in range(lax.axis_size(axis))])
+
+
+def joined(mine, other, bit, axis):
+    return jnp.where(bit == 0, jnp.stack([mine, other], axis), jnp.stack([other, mine], axis))
+
+
+def bits(axis):
+    me = lax.axis_index(axis)
+    return me % 2, me // 2
+
+
+def gather_col(x):
+    if lax.axis_size("col") != 4:
+        return lax.all_gather(x, "col", axis=0, tiled=True)
+    core, far = bits("col")
+    beside = flip(x, "col", 1)
+    across = flip(x, "col", 2)
+    corner = flip(across, "col", 1)
+    both = joined(joined(x, beside, core, 0), joined(across, corner, core, 0), far, 0)
+    return both.reshape((4 * x.shape[0],) + x.shape[1:])
+
+
+def scatter_col(x):
+    if lax.axis_size("col") != 4:
+        return wide(lax.psum_scatter(x, "col", scatter_dimension=0, tiled=True)), None
+    core, far = bits("col")
+    pieces = cut(cut(x, 4), 2)
+    other = flip(piece(pieces, 1 - core, 1), "col", 1)
+    halves = wide(piece(pieces, core, 1)) + wide(other)
+    sent = piece(halves, 1 - far).astype(x.dtype)
+    return piece(halves, far), sent
+
+
+def silu(value):
+    return jax.nn.silu(value).astype(jnp.bfloat16)
+
+
+def after(values, *earlier):
+    tied = lax.optimization_barrier((*values, *earlier))
+    return tied[: len(values)]
+
+
+def hidden_chunks(layer_one):
+    if lax.axis_size("row") != 2 or lax.axis_size("slab") != 4:
+        both = ("row", "slab")
+        return [
+            lax.all_gather(
+                silu(wide(lax.psum_scatter(layer_one(chunk, ()), both, scatter_dimension=0, tiled=True))),
+                both, axis=0, tiled=True,
+            )
+            for chunk in range(CHUNKS)
+        ]
+    row = lax.axis_index("row")
+    low, high = bits("slab")
+
+    def halves(first):
+        pieces = cut(first, 2)
+        return piece(pieces, row), piece(pieces, 1 - row)
+
+    def near(kept, other):
+        total = cut(cut((wide(kept) + wide(other)).astype(kept.dtype), 4), 2)
+        return piece(total, low, 1), piece(total, 1 - low, 1)
+
+    def distant(kept, other):
+        total = (wide(kept) + wide(other)).astype(kept.dtype)
+        return piece(total, high), piece(total, 1 - high)
+
+    def spread(kept, other):
+        kept, sent = distant(kept, other)
+        hidden = silu(wide(kept) + wide(flip(sent, "slab", 2)))
+        pair = joined(hidden, flip(hidden, "slab", 2), high, 0)
+        quad = joined(pair, flip(pair, "slab", 1), low, 1)
+        return hidden, quad.reshape((-1, quad.shape[-1]))
+
+    kept0, sent0 = halves(layer_one(0, ()))
+    other0 = flip(sent0, "row", 1)
+    kept1, sent1 = halves(layer_one(1, (sent0,)))
+    other1 = flip(sent1, "row", 1)
+    kept0, sent0 = near(kept0, other0)
+    other0 = flip(sent0, "slab", 1)
+    kept2, sent2 = halves(layer_one(2, (sent1, sent0)))
+    other2 = flip(sent2, "row", 1)
+    other0, other1 = after((other0, other1), sent2)
+    kept1, sent1 = near(kept1, other1)
+    other1 = flip(sent1, "slab", 1)
+    hidden0, quad0 = spread(kept0, other0)
+    hidden1, quad1 = spread(kept1, other1)
+    (other2,) = after((other2,), hidden0)
+    kept2, sent2 = near(kept2, other2)
+    hidden2, quad2 = spread(kept2, flip(sent2, "slab", 1))
+    return [
+        joined(quad, flip(quad, "row", 1), row, 0).reshape((-1, quad.shape[-1]))
+        for quad in (quad0, quad1, quad2)
+    ]
+
+
 def local(inputs, first_weight, second_weight):
-    full_input = lax.all_gather(inputs, "col", axis=0, tiled=True)
+    full_input = gather_col(inputs)
     height, width, depth = full_input.shape
     pixels = height * width
     flat = full_input.reshape(pixels, depth)
     out_first = first_weight.shape[3]
     out_second = second_weight.shape[3]
     size = out_first // CHUNKS
-    hiddens = []
-    for chunk in range(CHUNKS):
-        first = conv(flat, first_weight, height, width, 0, depth, chunk * size, size, None, jnp.bfloat16)
-        first = lax.psum_scatter(first, ("row", "slab"), scatter_dimension=0, tiled=True)
-        hidden = jax.nn.silu(first.astype(jnp.float32)).astype(jnp.bfloat16)
-        hiddens.append(lax.all_gather(hidden, ("row", "slab"), axis=0, tiled=True))
+
+    def layer_one(chunk, earlier):
+        (source,) = after((flat,), *earlier) if earlier else (flat,)
+        return conv(source, first_weight, height, width, 0, depth, chunk * size, size, None, jnp.bfloat16)
+
+    hiddens = hidden_chunks(layer_one)
     total = None
-    for chunk in range(CHUNKS):
-        last = chunk == CHUNKS - 1
-        total = conv(
-            hiddens[chunk], second_weight, height, width, chunk, size, 0, out_second, total,
-            jnp.bfloat16 if last else jnp.float32,
+    for chunk in range(CHUNKS - 1):
+        total = conv(hiddens[chunk], second_weight, height, width, chunk, size, 0, out_second, total, jnp.float32)
+    split = 512 if out_second % 256 == 0 and out_second > 512 else out_second
+    parts = []
+    for start, end in ((0, split), (split, out_second)):
+        if start == end:
+            continue
+        part = conv(
+            hiddens[-1], second_weight, height, width, CHUNKS - 1, size, start, end - start, total, jnp.bfloat16
         )
-    second = lax.psum_scatter(total, "col", scatter_dimension=0, tiled=True).astype(jnp.float32)
-    combined = inputs.astype(jnp.float32) + second.reshape(inputs.shape)
-    return combined.astype(jnp.bfloat16)
+        second, sent = scatter_col(part)
+        if sent is not None:
+            second = second + wide(flip(sent, "col", 2))
+            (total,) = after((total,), sent)
+        second = second.reshape(inputs.shape[:2] + (end - start,))
+        parts.append((wide(inputs[:, :, start:end]) + second).astype(jnp.bfloat16))
+    return jnp.concatenate(parts, axis=2)
 
 
 def solution(mesh):

time: 488 us -> 295 us (0.60)
  waiting for transfers between devices: 339 us -> 125 us
  starting transfers between devices: 0.47 us -> 21.1 us
  between operations: 13.5 us -> 0.37 us
  other arithmetic: 7.63 us -> 18.9 us
    reduce_scatter x4 -> x0, waiting for transfers between devices: 201 us -> none  [the longest x3 165 us: local(): lax.psum_scatter(first, ('row', 'slab'), scatter_dimension=0, tiled=True)]
    all_gather x4 -> x0, waiting for transfers between devices: 137 us -> none  [the longest x3 105 us: local(): hiddens.append(lax.all_gather(hidden, ('row', 'slab'), axis=0, tiled=True))]
    ppermute x0 -> x25, waiting for transfers between devices: none -> 125 us  [flip(): lax.ppermute(x, axis, [(i, i ^ bit) for i in range(lax.axis_size(axis))])]
    ppermute x0 -> x25, starting transfers between devices: none -> 21.1 us  [flip(): lax.ppermute(x, axis, [(i, i ^ bit) for i in range(lax.axis_size(axis))])]
    select_n x0 -> x15, other arithmetic: none -> 8.41 us  [joined(): jnp.where(bit == 0, jnp.stack([mine, other], axis), jnp.stack([other, min...]
    squeeze x0 -> x11, local copies, waits for them, and re-layouts: none -> 5.22 us  [piece(): return lax.dynamic_index_in_dim(pieces, index, axis, keepdims=False)]
    pallas_call x6 -> x7, Pallas kernels: 120 us -> 120 us  [conv(): pl.pallas_call(functools.partial(conv_kernel, height, width, total is not...]
  transfers between devices with their start and end apart: 8 -> 25, of which waited for: 8 -> 17; matrix products, arithmetic and copies ran while one was open for 1% -> 6% of each run, Pallas kernels for 16% -> 27%
where the time goes in v3:
time: 295 us; the launch traced here: 294 us
  waiting for transfers between devices  125 us (42%)
  Pallas kernels  120 us (41%)
  starting transfers between devices  21.1 us (7%)
  other arithmetic  18.9 us (6%)
  local copies, waits for them, and re-layouts  9.14 us (3%)
    ppermute x25, waiting for transfers between devices, flip(): lax.ppermute(x, axis, [(i, i ^ bit) for i in range(lax.axis_size(axis))])  125 us
    pallas_call x7, Pallas kernels, conv(): pl.pallas_call(functools.partial(conv_kernel, height, width, total is not...  120 us
    ppermute x25, starting transfers between devices, flip(): lax.ppermute(x, axis, [(i, i ^ bit) for i in range(lax.axis_size(axis))])  21.1 us
    select_n x15, other arithmetic, joined(): jnp.where(bit == 0, jnp.stack([mine, other], axis), jnp.stack([other, min...  8.41 us
  transfers between devices with their start and end apart: 25, of which 17 were waited for; matrix products, arithmetic and copies ran while one was open for 6% of the time, Pallas kernels for 27%

profile of v3, /device:TPU:0, one launch (start us, length us, event | category | flops | bytes accessed | tf_op | source)
XLA Modules:
  0.0 294.4 jit_solution(3199625035155290080)
XLA Ops:
  0.0 3.0 %collective-permute-start.1 = (bf16[8,64,768]{2,1,0:T(8,128)(2,1)}, bf16[8,64,768]{2,1,0:T(8,128)(2,1)S(1)}, u32[]{:S(2)}, u32[]{:S(2)}) collective-permute-start(bf16[8,64,768]{2,1,0:T(8,128)(2,1)} %param.3), channel_id=1, source_target_pairs={{0,8},{4,12},{8,0},{12,4},{1,9},{5,13},{9,1},{13,5},{2,10},{6,14},... | collective-permute-start | bytes 2359304 | tf_op jit(solution)/shard_map/ppermute | solution.py:105
  3.0 17.7 %collective-permute-done.1 = bf16[8,64,768]{2,1,0:T(8,128)(2,1)S(1)} collective-permute-done((bf16[8,64,768]{2,1,0:T(8,128)(2,1)}, bf16[8,64,768]{2,1,0:T(8,128)(2,1)S(1)}, u32[]{:S(2)}, u32[]{:S(2)}) %collective-permute-start.1) | collective-permute-done | bytes 786464 | tf_op jit(solution)/shard_map/ppermute | solution.py:105
  20.7 1.6 maximum_select_fusion.4
  23.8 19.0 %shard_map.37 = bf16[2048,512]{1,0:T(8,128)(2,1)S(1)} custom-call(bf16[2048,768]{1,0:T(8,128)(2,1)S(1)} %bitcast.125, bf16[3,3,768,1536]{3,2,1,0:T(8,128)(2,1)} %w_ref.9), custom_call_target="tpu_custom_call" | custom-call | flops 14495514624 | bytes 12320768 | tf_op jit(solution)/shard_map/pallas_call | solution.py:74
  42.9 1.8 collective-permute-start.3
  44.6 19.0 %shard_map.38 = bf16[2048,512]{1,0:T(8,128)(2,1)S(1)} custom-call(bf16[2048,768]{1,0:T(8,128)(2,1)S(1)} %bitcast.126, bf16[3,3,768,1536]{3,2,1,0:T(8,128)(2,1)} %w_ref.9), custom_call_target="tpu_custom_call" | custom-call | flops 14495514624 | bytes 12320768 | tf_op jit(solution)/shard_map/pallas_call | solution.py:74
  63.6 1.1 dynamic-slice_bitcast_fusion.2
  65.1 3.7 %collective-permute-done.3 = bf16[1024,512]{1,0:T(8,128)(2,1)S(1)} collective-permute-done((bf16[1024,512]{1,0:T(8,128)(2,1)S(1)}, bf16[1024,512]{1,0:T(8,128)(2,1)S(1)}, u32[]{:S(2)}, u32[]{:S(2)}) %collective-permute-start.3) | collective-permute-done | bytes 1048608 | tf_op jit(solution)/shard_map/ppermute | solution.py:105
  69.9 2.0 collective-permute-start.5
  71.9 19.1 %shard_map.39 = bf16[2048,512]{1,0:T(8,128)(2,1)S(1)} custom-call(bf16[2048,768]{1,0:T(8,128)(2,1)S(1)} %bitcast.127, bf16[3,3,768,1536]{3,2,1,0:T(8,128)(2,1)} %w_ref.9), custom_call_target="tpu_custom_call" | custom-call | flops 14495514624 | bytes 12320768 | tf_op jit(solution)/shard_map/pallas_call | solution.py:74
  91.0 1.0 dynamic-slice_bitcast_fusion.1
  92.1 1.5 collective-permute-start.4
  93.6 1.3 fusion.5
  94.9 2.7 collective-permute-start.7
  97.6 1.5 fusion
  99.7 8.0 %collective-permute-done.7 = bf16[256,512]{1,0:T(8,128)(2,1)S(1)} collective-permute-done((bf16[256,512]{1,0:T(8,128)(2,1)S(1)}, bf16[256,512]{1,0:T(8,128)(2,1)S(1)}, u32[]{:S(2)}, u32[]{:S(2)}) %collective-permute-start.7) | collective-permute-done | bytes 262176 | tf_op jit(solution)/shard_map/ppermute | solution.py:105
  108.0 7.7 %collective-permute-done.4 = bf16[1024,512]{1,0:T(8,128)(2,1)} collective-permute-done((bf16[1024,512]{1,0:T(8,128)(2,1)}, bf16[1024,512]{1,0:T(8,128)(2,1)}, u32[]{:S(2)}, u32[]{:S(2)}) %collective-permute-start.4) | collective-permute-done | bytes 1048608 | tf_op jit(solution)/shard_map/ppermute | solution.py:105
  115.7 1.5 fusion.1
  117.6 8.4 %collective-permute-done.13 = bf16[2,256,512]{2,1,0:T(8,128)(2,1)S(1)} collective-permute-done((bf16[2,256,512]{2,1,0:T(8,128)(2,1)S(1)}, bf16[2,256,512]{2,1,0:T(8,128)(2,1)S(1)}, u32[]{:S(2)}, u32[]{:S(2)}) %collective-permute-start.13) | collective-permute-done | bytes 524320 | tf_op jit(solution)/shard_map/ppermute | solution.py:105
  126.5 13.5 %collective-permute-done.8 = bf16[2,256,512]{2,1,0:T(8,128)(2,1)S(1)} collective-permute-done((bf16[2,256,512]{2,1,0:T(8,128)(2,1)S(1)}, bf16[2,256,512]{2,1,0:T(8,128)(2,1)S(1)}, u32[]{:S(2)}, u32[]{:S(2)}) %collective-permute-start.8) | collective-permute-done | bytes 524320 | tf_op jit(solution)/shard_map/ppermute | solution.py:105
  140.4 3.0 %collective-permute-start.15 = (bf16[256,512]{1,0:T(8,128)(2,1)S(1)}, bf16[256,512]{1,0:T(8,128)(2,1)S(1)}, u32[]{:S(2)}, u32[]{:S(2)}) collective-permute-start(bf16[256,512]{1,0:T(8,128)(2,1)S(1)} %multiply_convert_fusion), channel_id=1, source_target_pairs={{0,2},{1,3},{2,0},{3,1},{4,6},{5,7},{6,4},{7,5},{8,10},{9,11},{10,... | collective-permute-start | bytes 786440 | tf_op jit(solution)/shard_map/ppermute | solution.py:105
  143.4 12.8 %collective-permute-done.19 = bf16[2,256,512]{2,1,0:T(8,128)(2,1)S(1)} collective-permute-done((bf16[2,256,512]{2,1,0:T(8,128)(2,1)S(1)}, bf16[2,256,512]{2,1,0:T(8,128)(2,1)S(1)}, u32[]{:S(2)}, u32[]{:S(2)}) %collective-permute-start.19) | collective-permute-done | bytes 524320 | tf_op jit(solution)/shard_map/ppermute | solution.py:105
  156.4 1.1 collective-permute-start.20
  157.5 9.2 %collective-permute-done.9 = bf16[256,512]{1,0:T(8,128)(2,1)S(1)} collective-permute-done((bf16[256,512]{1,0:T(8,128)(2,1)S(1)}, bf16[256,512]{1,0:T(8,128)(2,1)S(1)}, u32[]{:S(2)}, u32[]{:S(2)}) %collective-permute-start.9) | collective-permute-done | bytes 262176 | tf_op jit(solution)/shard_map/ppermute | solution.py:105
  166.9 5.2 %collective-permute-done.15 = bf16[256,512]{1,0:T(8,128)(2,1)S(1)} collective-permute-done((bf16[256,512]{1,0:T(8,128)(2,1)S(1)}, bf16[256,512]{1,0:T(8,128)(2,1)S(1)}, u32[]{:S(2)}, u32[]{:S(2)}) %collective-permute-start.15) | collective-permute-done | bytes 262176 | tf_op jit(solution)/shard_map/ppermute | solution.py:105
  172.1 0.9 maximum_select_fusion.11
  173.0 1.9 collective-permute-done.10
  176.0 12.2 %collective-permute-done.16 = bf16[2,256,512]{2,1,0:T(8,128)(2,1)} collective-permute-done((bf16[2,256,512]{2,1,0:T(8,128)(2,1)}, bf16[2,256,512]{2,1,0:T(8,128)(2,1)}, u32[]{:S(2)}, u32[]{:S(2)}) %collective-permute-start.16) | collective-permute-done | bytes 524320 | tf_op jit(solution)/shard_map/ppermute | solution.py:105
  188.2 1.4 maximum_select_fusion.7
  190.3 7.1 %collective-permute-done.11 = bf16[2,256,512]{2,1,0:T(8,128)(2,1)} collective-permute-done((bf16[2,256,512]{2,1,0:T(8,128)(2,1)}, bf16[2,256,512]{2,1,0:T(8,128)(2,1)}, u32[]{:S(2)}, u32[]{:S(2)}) %collective-permute-start.11) | collective-permute-done | bytes 524320 | tf_op jit(solution)/shard_map/ppermute | solution.py:105
  197.4 1.4 maximum_select_fusion.6
  199.7 19.7 %shard_map.40.rest_0_ = f32[2048,768]{1,0:T(8,128)} custom-call(bf16[2048,512]{1,0:T(8,128)(2,1)S(1)} %bitcast.137, bf16[3,3,1536,768]{3,2,1,0:T(8,128)(2,1)} %w_ref.13), custom_call_target="tpu_custom_call" | custom-call | flops 14495514624 | bytes 12320768 | tf_op jit(solution)/shard_map/pallas_call | solution.py:74
  219.8 20.5 %shard_map.41.rest_0_ = f32[2048,768]{1,0:T(8,128)} custom-call(bf16[2048,512]{1,0:T(8,128)(2,1)S(1)} %bitcast.136, bf16[3,3,1536,768]{3,2,1,0:T(8,128)(2,1)} %w_ref.13, f32[2048,768]{1,0:T(8,128)} %shard_map.40.rest_0_), custom_call_target="tpu_custom_call" | custom-call | flops 14495514624 | bytes 12320768 | tf_op jit(solution)/shard_map/pallas_call | solution.py:74
  240.6 13.9 %shard_map.42 = bf16[2048,512]{1,0:T(8,128)(2,1)S(1)} custom-call(bf16[2048,512]{1,0:T(8,128)(2,1)S(1)} %bitcast.121, bf16[3,3,1536,768]{3,2,1,0:T(8,128)(2,1)} %w_ref.13, f32[2048,768]{1,0:T(8,128)} %shard_map.41.rest_0_), custom_call_target="tpu_custom_call" | custom-call | flops 9663676416 | bytes 8912896 | tf_op jit(solution)/shard_map/pallas_call | solution.py:74
  254.5 1.4 copy-done
  255.9 1.1 dynamic-slice_bitcast_fusion
  257.0 2.9 collective-permute-done.21
  259.9 1.5 convert_add_fusion
  261.4 1.4 copy-done.3
  262.8 0.9 fusion.6
  263.8 8.5 %shard_map.43 = bf16[2048,256]{1,0:T(8,128)(2,1)S(1)} custom-call(bf16[2048,512]{1,0:T(8,128)(2,1)S(1)} %bitcast.122, bf16[3,3,1536,768]{3,2,1,0:T(8,128)(2,1)} %w_ref.13, f32[2048,768]{1,0:T(8,128)} %shard_map.41.rest_0_), custom_call_target="tpu_custom_call" | custom-call | flops 4831838208 | bytes 5505024 | tf_op jit(solution)/shard_map/pallas_call | solution.py:74
  273.3 1.6 collective-permute-start.22
  275.4 1.1 convert_add_fusion.4
  276.6 1.6 collective-permute-start.24
  278.2 10.1 %collective-permute-done.22 = bf16[512,512]{1,0:T(8,128)(2,1)} collective-permute-done((bf16[512,512]{1,0:T(8,128)(2,1)}, bf16[512,512]{1,0:T(8,128)(2,1)}, u32[]{:S(2)}, u32[]{:S(2)}) %collective-permute-start.22) | collective-permute-done | bytes 524320 | tf_op jit(solution)/shard_map/ppermute | solution.py:105
  288.4 1.2 bitcast_add_fusion
  289.8 3.6 %collective-permute-done.24 = bf16[512,256]{1,0:T(8,128)(2,1)S(1)} collective-permute-done((bf16[512,256]{1,0:T(8,128)(2,1)S(1)}, bf16[512,256]{1,0:T(8,128)(2,1)S(1)}, u32[]{:S(2)}, u32[]{:S(2)}) %collective-permute-start.24) | collective-permute-done | bytes 262176 | tf_op jit(solution)/shard_map/ppermute | solution.py:105
  293.5 0.9 pad_maximum_fusion
  (67 shorter events, 10.9 us)
Async XLA Ops:
  0.0 20.7 %collective-permute-start.1 = (bf16[8,64,768]{2,1,0:T(8,128)(2,1)}, bf16[8,64,768]{2,1,0:T(8,128)(2,1)S(1)}, u32[]{:S(2)}, u32[]{:S(2)}) collective-permute-start(bf16[8,64,768]{2,1,0:T(8,128)(2,1)} %param.3), channel_id=1, source_target_pairs={{0,8},{4,12},{8,0},{12,4},{1,9},{5,13},{9,1},{13,5},{2,10},{6,14},... | collective-permute-start | bytes 2359304 | tf_op jit(solution)/shard_map/ppermute | solution.py:105
  3.0 17.8 %collective-permute-start = (bf16[8,64,768]{2,1,0:T(8,128)(2,1)}, bf16[8,64,768]{2,1,0:T(8,128)(2,1)S(1)}, u32[]{:S(2)}, u32[]{:S(2)}) collective-permute-start(bf16[8,64,768]{2,1,0:T(8,128)(2,1)} %param.3), channel_id=1, source_target_pairs={{0,4},{4,0},{8,12},{12,8},{1,5},{5,1},{9,13},{13,9},{2,6},{6,2},{1... | collective-permute-start | bytes 2359304 | tf_op jit(solution)/shard_map/ppermute | solution.py:105
  20.7 2.3 collective-permute-start.2
  42.9 25.9 %collective-permute-start.3 = (bf16[1024,512]{1,0:T(8,128)(2,1)S(1)}, bf16[1024,512]{1,0:T(8,128)(2,1)S(1)}, u32[]{:S(2)}, u32[]{:S(2)}) collective-permute-start(bf16[1024,512]{1,0:T(8,128)(2,1)S(1)} %dynamic-slice_bitcast_fusion.3), channel_id=1, source_target_pairs={{0,16},{16,0},{1,17},{17,1},{2,18},{18,2},{3,19},{19,3},{4,20},{20... | collective-permute-start | bytes 3145736 | tf_op jit(solution)/shard_map/ppermute | solution.py:105
  63.6 5.4 %copy-start.1 = (bf16[2048,512]{1,0:T(8,128)(2,1)}, bf16[2048,512]{1,0:T(8,128)(2,1)S(1)}, u32[]{:S(2)}) copy-start(bf16[2048,512]{1,0:T(8,128)(2,1)S(1)} %shard_map.38) | copy-start | bytes 6291460
  64.8 28.8 %collective-permute-start.6 = (bf16[1024,512]{1,0:T(8,128)(2,1)}, bf16[1024,512]{1,0:T(8,128)(2,1)}, u32[]{:S(2)}, u32[]{:S(2)}) collective-permute-start(bf16[1024,512]{1,0:T(8,128)(2,1)} %dynamic-slice_bitcast_fusion.2), channel_id=1, source_target_pairs={{0,16},{16,0},{1,17},{17,1},{2,18},{18,2},{3,19},{19,3},{4,20},{20... | collective-permute-start | bytes 3145736 | tf_op jit(solution)/shard_map/ppermute | solution.py:105
  69.9 23.7 %collective-permute-start.5 = (bf16[2,256,512]{2,1,0:T(8,128)(2,1)}, bf16[2,256,512]{2,1,0:T(8,128)(2,1)}, u32[]{:S(2)}, u32[]{:S(2)}) collective-permute-start(bf16[2,256,512]{2,1,0:T(8,128)(2,1)} %dynamic-slice_bitcast_fusion.7), channel_id=1, source_target_pairs={{0,1},{1,0},{2,3},{3,2},{4,5},{5,4},{6,7},{7,6},{8,9},{9,8},{10,11... | collective-permute-start | bytes 1572872 | tf_op jit(solution)/shard_map/ppermute | solution.py:105
  92.1 23.6 %collective-permute-start.4 = (bf16[1024,512]{1,0:T(8,128)(2,1)}, bf16[1024,512]{1,0:T(8,128)(2,1)}, u32[]{:S(2)}, u32[]{:S(2)}) collective-permute-start(bf16[1024,512]{1,0:T(8,128)(2,1)} %dynamic-slice_bitcast_fusion.1), channel_id=1, source_target_pairs={{0,16},{16,0},{1,17},{17,1},{2,18},{18,2},{3,19},{19,3},{4,20},{20... | collective-permute-start | bytes 3145736 | tf_op jit(solution)/shard_map/ppermute | solution.py:105
  93.6 4.0 %copy-start.2 = (bf16[2048,512]{1,0:T(8,128)(2,1)S(1)}, bf16[2048,512]{1,0:T(8,128)(2,1)}, u32[]{:S(2)}) copy-start(bf16[2048,512]{1,0:T(8,128)(2,1)} %copy-done.1) | copy-start | bytes 6291460
  94.9 12.7 %collective-permute-start.7 = (bf16[256,512]{1,0:T(8,128)(2,1)S(1)}, bf16[256,512]{1,0:T(8,128)(2,1)S(1)}, u32[]{:S(2)}, u32[]{:S(2)}) collective-permute-start(bf16[256,512]{1,0:T(8,128)(2,1)S(1)} %dynamic-slice_bitcast_fusion.10), channel_id=1, source_target_pairs={{0,2},{1,3},{2,0},{3,1},{4,6},{5,7},{6,4},{7,5},{8,10},{9,11},{10,... | collective-permute-start | bytes 786440 | tf_op jit(solution)/shard_map/ppermute | solution.py:105
  99.2 26.8 %collective-permute-start.13 = (bf16[2,256,512]{2,1,0:T(8,128)(2,1)S(1)}, bf16[2,256,512]{2,1,0:T(8,128)(2,1)S(1)}, u32[]{:S(2)}, u32[]{:S(2)}) collective-permute-start(bf16[2,256,512]{2,1,0:T(8,128)(2,1)S(1)} %dynamic-slice_bitcast_fusion.5), channel_id=1, source_target_pairs={{0,1},{1,0},{2,3},{3,2},{4,5},{5,4},{6,7},{7,6},{8,9},{9,8},{10,11... | collective-permute-start | bytes 1572872 | tf_op jit(solution)/shard_map/ppermute | solution.py:105
  107.8 18.4 %collective-permute-start.18 = (bf16[256,512]{1,0:T(8,128)(2,1)S(1)}, bf16[256,512]{1,0:T(8,128)(2,1)S(1)}, u32[]{:S(2)}, u32[]{:S(2)}) collective-permute-start(bf16[256,512]{1,0:T(8,128)(2,1)S(1)} %multiply_convert_fusion.2), channel_id=1, source_target_pairs={{0,2},{1,3},{2,0},{3,1},{4,6},{5,7},{6,4},{7,5},{8,10},{9,11},{10,... | collective-permute-start | bytes 786440 | tf_op jit(solution)/shard_map/ppermute | solution.py:105
  117.2 22.7 %collective-permute-start.8 = (bf16[2,256,512]{2,1,0:T(8,128)(2,1)S(1)}, bf16[2,256,512]{2,1,0:T(8,128)(2,1)S(1)}, u32[]{:S(2)}, u32[]{:S(2)}) collective-permute-start(bf16[2,256,512]{2,1,0:T(8,128)(2,1)S(1)} %dynamic-slice_bitcast_fusion.6), channel_id=1, source_target_pairs={{0,1},{1,0},{2,3},{3,2},{4,5},{5,4},{6,7},{7,6},{8,9},{9,8},{10,11... | collective-permute-start | bytes 1572872 | tf_op jit(solution)/shard_map/ppermute | solution.py:105
  126.1 14.1 %collective-permute-start.14 = (bf16[256,512]{1,0:T(8,128)(2,1)S(1)}, bf16[256,512]{1,0:T(8,128)(2,1)S(1)}, u32[]{:S(2)}, u32[]{:S(2)}) collective-permute-start(bf16[256,512]{1,0:T(8,128)(2,1)S(1)} %dynamic-slice_bitcast_fusion.8), channel_id=1, source_target_pairs={{0,2},{1,3},{2,0},{3,1},{4,6},{5,7},{6,4},{7,5},{8,10},{9,11},{10,... | collective-permute-start | bytes 786440 | tf_op jit(solution)/shard_map/ppermute | solution.py:105
  126.3 29.8 %collective-permute-start.19 = (bf16[2,256,512]{2,1,0:T(8,128)(2,1)S(1)}, bf16[2,256,512]{2,1,0:T(8,128)(2,1)S(1)}, u32[]{:S(2)}, u32[]{:S(2)}) collective-permute-start(bf16[2,256,512]{2,1,0:T(8,128)(2,1)S(1)} %maximum_select_fusion.12), channel_id=1, source_target_pairs={{0,1},{1,0},{2,3},{3,2},{4,5},{5,4},{6,7},{7,6},{8,9},{9,8},{10,11... | collective-permute-start | bytes 1572872 | tf_op jit(solution)/shard_map/ppermute | solution.py:105
  140.2 26.5 %collective-permute-start.9 = (bf16[256,512]{1,0:T(8,128)(2,1)S(1)}, bf16[256,512]{1,0:T(8,128)(2,1)S(1)}, u32[]{:S(2)}, u32[]{:S(2)}) collective-permute-start(bf16[256,512]{1,0:T(8,128)(2,1)S(1)} %dynamic-slice_bitcast_fusion.9), channel_id=1, source_target_pairs={{0,2},{1,3},{2,0},{3,1},{4,6},{5,7},{6,4},{7,5},{8,10},{9,11},{10,... | collective-permute-start | bytes 786440 | tf_op jit(solution)/shard_map/ppermute | solution.py:105
  140.4 31.7 %collective-permute-start.15 = (bf16[256,512]{1,0:T(8,128)(2,1)S(1)}, bf16[256,512]{1,0:T(8,128)(2,1)S(1)}, u32[]{:S(2)}, u32[]{:S(2)}) collective-permute-start(bf16[256,512]{1,0:T(8,128)(2,1)S(1)} %multiply_convert_fusion), channel_id=1, source_target_pairs={{0,2},{1,3},{2,0},{3,1},{4,6},{5,7},{6,4},{7,5},{8,10},{9,11},{10,... | collective-permute-start | bytes 786440 | tf_op jit(solution)/shard_map/ppermute | solution.py:105
  156.4 42.9 %collective-permute-start.20 = (bf16[1024,512]{1,0:T(8,128)(2,1)S(1)}, bf16[1024,512]{1,0:T(8,128)(2,1)S(1)}, u32[]{:S(2)}, u32[]{:S(2)}) collective-permute-start(bf16[1024,512]{1,0:T(8,128)(2,1)S(1)} %bitcast.140), channel_id=1, source_target_pairs={{0,16},{16,0},{1,17},{17,1},{2,18},{18,2},{3,19},{19,3},{4,20},{20... | collective-permute-start | bytes 3145736 | tf_op jit(solution)/shard_map/ppermute | solution.py:105
  166.8 8.1 %collective-permute-start.10 = (bf16[256,512]{1,0:T(8,128)(2,1)S(1)}, bf16[256,512]{1,0:T(8,128)(2,1)S(1)}, u32[]{:S(2)}, u32[]{:S(2)}) collective-permute-start(bf16[256,512]{1,0:T(8,128)(2,1)S(1)} %multiply_convert_fusion.1), channel_id=1, source_target_pairs={{0,2},{1,3},{2,0},{3,1},{4,6},{5,7},{6,4},{7,5},{8,10},{9,11},{10,... | collective-permute-start | bytes 786440 | tf_op jit(solution)/shard_map/ppermute | solution.py:105
  173.0 15.2 %collective-permute-start.16 = (bf16[2,256,512]{2,1,0:T(8,128)(2,1)}, bf16[2,256,512]{2,1,0:T(8,128)(2,1)}, u32[]{:S(2)}, u32[]{:S(2)}) collective-permute-start(bf16[2,256,512]{2,1,0:T(8,128)(2,1)} %maximum_select_fusion.11), channel_id=1, source_target_pairs={{0,1},{1,0},{2,3},{3,2},{4,5},{5,4},{6,7},{7,6},{8,9},{9,8},{10,11... | collective-permute-start | bytes 1572872 | tf_op jit(solution)/shard_map/ppermute | solution.py:105
  175.8 21.6 %collective-permute-start.11 = (bf16[2,256,512]{2,1,0:T(8,128)(2,1)}, bf16[2,256,512]{2,1,0:T(8,128)(2,1)}, u32[]{:S(2)}, u32[]{:S(2)}) collective-permute-start(bf16[2,256,512]{2,1,0:T(8,128)(2,1)} %maximum_select_fusion.9), channel_id=1, source_target_pairs={{0,1},{1,0},{2,3},{3,2},{4,5},{5,4},{6,7},{7,6},{8,9},{9,8},{10,11... | collective-permute-start | bytes 1572872 | tf_op jit(solution)/shard_map/ppermute | solution.py:105
  189.7 29.8 %collective-permute-start.17 = (bf16[1024,512]{1,0:T(8,128)(2,1)S(1)}, bf16[1024,512]{1,0:T(8,128)(2,1)S(1)}, u32[]{:S(2)}, u32[]{:S(2)}) collective-permute-start(bf16[1024,512]{1,0:T(8,128)(2,1)S(1)} %bitcast.142), channel_id=1, source_target_pairs={{0,16},{16,0},{1,17},{17,1},{2,18},{18,2},{3,19},{19,3},{4,20},{20... | collective-permute-start | bytes 3145736 | tf_op jit(solution)/shard_map/ppermute | solution.py:105
  198.8 41.5 %collective-permute-start.12 = (bf16[1024,512]{1,0:T(8,128)(2,1)S(1)}, bf16[1024,512]{1,0:T(8,128)(2,1)S(1)}, u32[]{:S(2)}, u32[]{:S(2)}) collective-permute-start(bf16[1024,512]{1,0:T(8,128)(2,1)S(1)} %bitcast.138), channel_id=1, source_target_pairs={{0,16},{16,0},{1,17},{17,1},{2,18},{18,2},{3,19},{19,3},{4,20},{20... | collective-permute-start | bytes 3145736 | tf_op jit(solution)/shard_map/ppermute | solution.py:105
  254.5 1.4 copy-start
  257.0 2.9 collective-permute-start.21
  261.4 1.4 copy-start.3
  272.3 16.1 %copy-start.4 = (f32[2,512,512]{2,1,0:T(8,128)S(1)}, f32[2,512,512]{2,1,0:T(8,128)}, u32[]{:S(2)}) copy-start(f32[2,512,512]{2,1,0:T(8,128)} %copy-done.3) | copy-start | bytes 6291460
  273.2 2.3 collective-permute-start.23
  273.3 15.1 %collective-permute-start.22 = (bf16[512,512]{1,0:T(8,128)(2,1)}, bf16[512,512]{1,0:T(8,128)(2,1)}, u32[]{:S(2)}, u32[]{:S(2)}) collective-permute-start(bf16[512,512]{1,0:T(8,128)(2,1)} %fusion.6), channel_id=1, source_target_pairs={{0,8},{4,12},{8,0},{12,4},{1,9},{5,13},{9,1},{13,5},{2,10},{6,14},... | collective-permute-start | bytes 1572872 | tf_op jit(solution)/shard_map/ppermute | solution.py:105
  276.6 13.0 %copy-start.5 = (bf16[8,64,768]{2,1,0:T(8,128)(2,1)S(1)}, bf16[8,64,768]{2,1,0:T(8,128)(2,1)}, u32[]{:S(2)}) copy-start(bf16[8,64,768]{2,1,0:T(8,128)(2,1)} %param.3) | copy-start | bytes 2359300
  276.6 16.7 %collective-permute-start.24 = (bf16[512,256]{1,0:T(8,128)(2,1)S(1)}, bf16[512,256]{1,0:T(8,128)(2,1)S(1)}, u32[]{:S(2)}, u32[]{:S(2)}) collective-permute-start(bf16[512,256]{1,0:T(8,128)(2,1)S(1)} %fusion.8), channel_id=1, source_target_pairs={{0,8},{4,12},{8,0},{12,4},{1,9},{5,13},{9,1},{13,5},{2,10},{6,14},... | collective-permute-start | bytes 786440 | tf_op jit(solution)/shard_map/ppermute | solution.py:105

commit v4 on v3

--- a/solution.py
+++ b/solution.py
@@ -148,7 +148,7 @@
 def hidden_chunks(layer_one):
     if lax.axis_size("row") != 2 or lax.axis_size("slab") != 4:
         both = ("row", "slab")
-        return [
+        return (), (), [
             lax.all_gather(
                 silu(wide(lax.psum_scatter(layer_one(chunk, ()), both, scatter_dimension=0, tiled=True))),
                 both, axis=0, tiled=True,
@@ -190,10 +190,10 @@
     other1 = flip(sent1, "slab", 1)
     hidden0, quad0 = spread(kept0, other0)
     hidden1, quad1 = spread(kept1, other1)
-    (other2,) = after((other2,), hidden0)
+    (other2,) = after((other2,), quad0, hidden1)
     kept2, sent2 = near(kept2, other2)
     hidden2, quad2 = spread(kept2, flip(sent2, "slab", 1))
-    return [
+    return (hidden2,), (quad2,), [
         joined(quad, flip(quad, "row", 1), row, 0).reshape((-1, quad.shape[-1]))
         for quad in (quad0, quad1, quad2)
     ]
@@ -212,22 +212,27 @@
         (source,) = after((flat,), *earlier) if earlier else (flat,)
         return conv(source, first_weight, height, width, 0, depth, chunk * size, size, None, jnp.bfloat16)
 
-    hiddens = hidden_chunks(layer_one)
+    *waits, hiddens = hidden_chunks(layer_one)
     total = None
     for chunk in range(CHUNKS - 1):
-        total = conv(hiddens[chunk], second_weight, height, width, chunk, size, 0, out_second, total, jnp.float32)
+        (source,) = after((hiddens[chunk],), *waits[chunk]) if waits[chunk] else (hiddens[chunk],)
+        total = conv(source, second_weight, height, width, chunk, size, 0, out_second, total, jnp.float32)
     split = 512 if out_second % 256 == 0 and out_second > 512 else out_second
-    parts = []
+    parts, came = [], ()
     for start, end in ((0, split), (split, out_second)):
         if start == end:
             continue
         part = conv(
             hiddens[-1], second_weight, height, width, CHUNKS - 1, size, start, end - start, total, jnp.bfloat16
         )
+        if came:
+            (part,) = after((part,), *came)
         second, sent = scatter_col(part)
         if sent is not None:
-            second = second + wide(flip(sent, "col", 2))
+            got = flip(sent, "col", 2)
+            second = second + wide(got)
             (total,) = after((total,), sent)
+            came = (got,)
         second = second.reshape(inputs.shape[:2] + (end - start,))
         parts.append((wide(inputs[:, :, start:end]) + second).astype(jnp.bfloat16))
     return jnp.concatenate(parts, axis=2)

time: 295 us -> 290 us (0.983)
  waiting for transfers between devices: 125 us -> 103 us
  starting transfers between devices: 21.1 us -> 37.2 us
    ppermute x25, waiting for transfers between devices: 125 us -> 103 us  [flip(): lax.ppermute(x, axis, [(i, i ^ bit) for i in range(lax.axis_size(axis))])]
    ppermute x25, starting transfers between devices: 21.1 us -> 37.2 us  [flip(): lax.ppermute(x, axis, [(i, i ^ bit) for i in range(lax.axis_size(axis))])]
  transfers between devices with their start and end apart: 25 -> 25, of which waited for: 17 -> 14; matrix products, arithmetic and copies ran while one was open for 6% -> 6% of each run, Pallas kernels for 27% -> 30%
where the time goes in v4:
time: 290 us; the launch traced here: 289 us
  Pallas kernels  120 us (41%)
  waiting for transfers between devices  103 us (36%)
  starting transfers between devices  37.2 us (13%)
  other arithmetic  21.2 us (7%)
  local copies, waits for them, and re-layouts  7.9 us (3%)
    pallas_call x7, Pallas kernels, conv(): pl.pallas_call(functools.partial(conv_kernel, height, width, total is not...  120 us
    ppermute x25, waiting for transfers between devices, flip(): lax.ppermute(x, axis, [(i, i ^ bit) for i in range(lax.axis_size(axis))])  103 us
    ppermute x25, starting transfers between devices, flip(): lax.ppermute(x, axis, [(i, i ^ bit) for i in range(lax.axis_size(axis))])  37.2 us
    select_n x15, other arithmetic, joined(): jnp.where(bit == 0, jnp.stack([mine, other], axis), jnp.stack([other, min...  10.8 us
  transfers between devices with their start and end apart: 25, of which 14 were waited for; matrix products, arithmetic and copies ran while one was open for 6% of the time, Pallas kernels for 30%

profile of v4, /device:TPU:0, one launch (start us, length us, event | category | flops | bytes accessed | tf_op | source)
XLA Modules:
  0.0 289.3 jit_solution(5417136875947891762)
XLA Ops:
  0.0 3.0 %collective-permute-start.1 = (bf16[8,64,768]{2,1,0:T(8,128)(2,1)}, bf16[8,64,768]{2,1,0:T(8,128)(2,1)S(1)}, u32[]{:S(2)}, u32[]{:S(2)}) collective-permute-start(bf16[8,64,768]{2,1,0:T(8,128)(2,1)} %param.3), channel_id=1, source_target_pairs={{0,8},{4,12},{8,0},{12,4},{1,9},{5,13},{9,1},{13,5},{2,10},{6,14},... | collective-permute-start | bytes 2359304 | tf_op jit(solution)/shard_map/ppermute | solution.py:105
  3.0 17.7 %collective-permute-done.1 = bf16[8,64,768]{2,1,0:T(8,128)(2,1)S(1)} collective-permute-done((bf16[8,64,768]{2,1,0:T(8,128)(2,1)}, bf16[8,64,768]{2,1,0:T(8,128)(2,1)S(1)}, u32[]{:S(2)}, u32[]{:S(2)}) %collective-permute-start.1) | collective-permute-done | bytes 786464 | tf_op jit(solution)/shard_map/ppermute | solution.py:105
  20.7 1.6 maximum_select_fusion.4
  23.8 19.0 %shard_map.37 = bf16[2048,512]{1,0:T(8,128)(2,1)S(1)} custom-call(bf16[2048,768]{1,0:T(8,128)(2,1)S(1)} %bitcast.125, bf16[3,3,768,1536]{3,2,1,0:T(8,128)(2,1)} %w_ref.9), custom_call_target="tpu_custom_call" | custom-call | flops 14495514624 | bytes 12320768 | tf_op jit(solution)/shard_map/pallas_call | solution.py:74
  42.9 1.8 collective-permute-start.3
  44.6 19.0 %shard_map.38 = bf16[2048,512]{1,0:T(8,128)(2,1)S(1)} custom-call(bf16[2048,768]{1,0:T(8,128)(2,1)S(1)} %bitcast.126, bf16[3,3,768,1536]{3,2,1,0:T(8,128)(2,1)} %w_ref.9), custom_call_target="tpu_custom_call" | custom-call | flops 14495514624 | bytes 12320768 | tf_op jit(solution)/shard_map/pallas_call | solution.py:74
  64.1 4.9 %collective-permute-done.3 = bf16[1024,512]{1,0:T(8,128)(2,1)S(1)} collective-permute-done((bf16[1024,512]{1,0:T(8,128)(2,1)S(1)}, bf16[1024,512]{1,0:T(8,128)(2,1)S(1)}, u32[]{:S(2)}, u32[]{:S(2)}) %collective-permute-start.3) | collective-permute-done | bytes 1048608 | tf_op jit(solution)/shard_map/ppermute | solution.py:105
  69.3 1.9 collective-permute-start.5
  71.1 19.1 %shard_map.39 = bf16[2048,512]{1,0:T(8,128)(2,1)S(1)} custom-call(bf16[2048,768]{1,0:T(8,128)(2,1)S(1)} %bitcast.127, bf16[3,3,768,1536]{3,2,1,0:T(8,128)(2,1)} %w_ref.9), custom_call_target="tpu_custom_call" | custom-call | flops 14495514624 | bytes 12320768 | tf_op jit(solution)/shard_map/pallas_call | solution.py:74
  91.5 2.6 collective-permute-start.7
  96.4 8.8 %collective-permute-done.7 = bf16[256,512]{1,0:T(8,128)(2,1)S(1)} collective-permute-done((bf16[256,512]{1,0:T(8,128)(2,1)S(1)}, bf16[256,512]{1,0:T(8,128)(2,1)S(1)}, u32[]{:S(2)}, u32[]{:S(2)}) %collective-permute-start.7) | collective-permute-done | bytes 262176 | tf_op jit(solution)/shard_map/ppermute | solution.py:105
  105.4 1.6 collective-permute-start.4
  107.0 12.1 %collective-permute-done.8 = bf16[256,512]{1,0:T(8,128)(2,1)} collective-permute-done((bf16[256,512]{1,0:T(8,128)(2,1)S(1)}, bf16[256,512]{1,0:T(8,128)(2,1)}, u32[]{:S(2)}, u32[]{:S(2)}) %collective-permute-start.8) | collective-permute-done | bytes 262176 | tf_op jit(solution)/shard_map/ppermute | solution.py:105
  119.1 1.9 maximum_select_fusion.9
  121.0 1.5 collective-permute-start.9
  122.5 1.2 fusion.4
  124.5 3.6 %collective-permute-start.11 = (bf16[256,512]{1,0:T(8,128)(2,1)S(1)}, bf16[256,512]{1,0:T(8,128)(2,1)}, u32[]{:S(2)}, u32[]{:S(2)}) collective-permute-start(bf16[256,512]{1,0:T(8,128)(2,1)S(1)} %dynamic-slice_bitcast_fusion.9), channel_id=1, source_target_pairs={{0,2},{1,3},{2,0},{3,1},{4,6},{5,7},{6,4},{7,5},{8,10},{9,11},{10,... | collective-permute-start | bytes 786440 | tf_op jit(solution)/shard_map/ppermute | solution.py:105
  128.1 1.1 fusion.7
  129.2 10.1 %collective-permute-done.11 = bf16[256,512]{1,0:T(8,128)(2,1)} collective-permute-done((bf16[256,512]{1,0:T(8,128)(2,1)S(1)}, bf16[256,512]{1,0:T(8,128)(2,1)}, u32[]{:S(2)}, u32[]{:S(2)}) %collective-permute-start.11) | collective-permute-done | bytes 262176 | tf_op jit(solution)/shard_map/ppermute | solution.py:105
  139.3 1.2 multiply_convert_fusion.1
  140.5 1.4 maximum_select_fusion.6
  142.0 1.5 fusion.1
  143.5 4.4 %collective-permute-start.12 = (bf16[2,256,512]{2,1,0:T(8,128)(2,1)S(1)}, bf16[2,256,512]{2,1,0:T(8,128)(2,1)S(1)}, u32[]{:S(2)}, u32[]{:S(2)}) collective-permute-start(bf16[2,256,512]{2,1,0:T(8,128)(2,1)S(1)} %dynamic-slice_bitcast_fusion.5), channel_id=1, source_target_pairs={{0,1},{1,0},{2,3},{3,2},{4,5},{5,4},{6,7},{7,6},{8,9},{9,8},{10,11... | collective-permute-start | bytes 1572872 | tf_op jit(solution)/shard_map/ppermute | solution.py:105
  148.5 1.5 collective-permute-start.20
  150.0 13.9 %collective-permute-done.17 = bf16[256,512]{1,0:T(8,128)(2,1)S(1)} collective-permute-done((bf16[256,512]{1,0:T(8,128)(2,1)S(1)}, bf16[256,512]{1,0:T(8,128)(2,1)S(1)}, u32[]{:S(2)}, u32[]{:S(2)}) %collective-permute-start.17) | collective-permute-done | bytes 262176 | tf_op jit(solution)/shard_map/ppermute | solution.py:105
  164.8 1.3 collective-permute-start.18
  166.3 2.1 collective-permute-start.13
  168.5 12.6 %collective-permute-done.13 = bf16[256,512]{1,0:T(8,128)(2,1)} collective-permute-done((bf16[256,512]{1,0:T(8,128)(2,1)S(1)}, bf16[256,512]{1,0:T(8,128)(2,1)}, u32[]{:S(2)}, u32[]{:S(2)}) %collective-permute-start.13) | collective-permute-done | bytes 262176 | tf_op jit(solution)/shard_map/ppermute | solution.py:105
  182.2 3.6 %collective-permute-start.14 = (bf16[256,512]{1,0:T(8,128)(2,1)S(1)}, bf16[256,512]{1,0:T(8,128)(2,1)S(1)}, u32[]{:S(2)}, u32[]{:S(2)}) collective-permute-start(bf16[256,512]{1,0:T(8,128)(2,1)S(1)} %multiply_convert_fusion), channel_id=1, source_target_pairs={{0,2},{1,3},{2,0},{3,1},{4,6},{5,7},{6,4},{7,5},{8,10},{9,11},{10,... | collective-permute-start | bytes 786440 | tf_op jit(solution)/shard_map/ppermute | solution.py:105
  186.0 1.6 collective-permute-start.19
  187.5 1.9 maximum_select_fusion.3
  189.4 7.2 %collective-permute-done.14 = bf16[256,512]{1,0:T(8,128)(2,1)S(1)} collective-permute-done((bf16[256,512]{1,0:T(8,128)(2,1)S(1)}, bf16[256,512]{1,0:T(8,128)(2,1)S(1)}, u32[]{:S(2)}, u32[]{:S(2)}) %collective-permute-start.14) | collective-permute-done | bytes 262176 | tf_op jit(solution)/shard_map/ppermute | solution.py:105
  196.8 19.7 %shard_map.40.rest_0_ = f32[2048,768]{1,0:T(8,128)} custom-call(bf16[2048,512]{1,0:T(8,128)(2,1)S(1)} %bitcast.136, bf16[3,3,1536,768]{3,2,1,0:T(8,128)(2,1)} %w_ref.13), custom_call_target="tpu_custom_call" | custom-call | flops 14495514624 | bytes 12320768 | tf_op jit(solution)/shard_map/pallas_call | solution.py:74
  216.7 1.6 collective-permute-start.16
  218.6 20.4 %shard_map.41.rest_0_ = f32[2048,768]{1,0:T(8,128)} custom-call(bf16[2048,512]{1,0:T(8,128)(2,1)S(1)} %bitcast.137, bf16[3,3,1536,768]{3,2,1,0:T(8,128)(2,1)} %w_ref.13, f32[2048,768]{1,0:T(8,128)} %shard_map.40.rest_0_), custom_call_target="tpu_custom_call" | custom-call | flops 14495514624 | bytes 12320768 | tf_op jit(solution)/shard_map/pallas_call | solution.py:74
  239.0 1.1 collective-permute-done.16
  240.5 13.9 %shard_map.42 = bf16[2048,512]{1,0:T(8,128)(2,1)S(1)} custom-call(bf16[2048,512]{1,0:T(8,128)(2,1)S(1)} %bitcast.121, bf16[3,3,1536,768]{3,2,1,0:T(8,128)(2,1)} %w_ref.13, f32[2048,768]{1,0:T(8,128)} %shard_map.41.rest_0_), custom_call_target="tpu_custom_call" | custom-call | flops 9663676416 | bytes 8912896 | tf_op jit(solution)/shard_map/pallas_call | solution.py:74
  254.5 1.4 copy-done
  255.8 1.1 dynamic-slice_bitcast_fusion
  257.0 2.9 collective-permute-done.21
  259.8 1.5 convert_add_fusion
  261.5 1.3 copy-done.1
  262.8 1.5 collective-permute-start.22
  264.3 8.5 %shard_map.43 = bf16[2048,256]{1,0:T(8,128)(2,1)S(1)} custom-call(bf16[2048,512]{1,0:T(8,128)(2,1)S(1)} %bitcast.122, bf16[3,3,1536,768]{3,2,1,0:T(8,128)(2,1)} %w_ref.13, f32[2048,768]{1,0:T(8,128)} %shard_map.41.rest_0_), custom_call_target="tpu_custom_call" | custom-call | flops 4831838208 | bytes 5505024 | tf_op jit(solution)/shard_map/pallas_call | solution.py:74
  272.8 3.9 %collective-permute-done.22 = bf16[512,512]{1,0:T(8,128)(2,1)S(1)} collective-permute-done((bf16[512,512]{1,0:T(8,128)(2,1)S(1)}, bf16[512,512]{1,0:T(8,128)(2,1)S(1)}, u32[]{:S(2)}, u32[]{:S(2)}) %collective-permute-start.22) | collective-permute-done | bytes 524320 | tf_op jit(solution)/shard_map/ppermute | solution.py:105
  277.7 1.6 bitcast_add_fusion
  279.7 1.6 collective-permute-start.24
  281.5 6.8 %collective-permute-done.24 = bf16[512,256]{1,0:T(8,128)(2,1)S(1)} collective-permute-done((bf16[512,256]{1,0:T(8,128)(2,1)S(1)}, bf16[512,256]{1,0:T(8,128)(2,1)S(1)}, u32[]{:S(2)}, u32[]{:S(2)}) %collective-permute-start.24) | collective-permute-done | bytes 262176 | tf_op jit(solution)/shard_map/ppermute | solution.py:105
  (65 shorter events, 13.6 us)
Async XLA Ops:
  0.0 20.7 %collective-permute-start.1 = (bf16[8,64,768]{2,1,0:T(8,128)(2,1)}, bf16[8,64,768]{2,1,0:T(8,128)(2,1)S(1)}, u32[]{:S(2)}, u32[]{:S(2)}) collective-permute-start(bf16[8,64,768]{2,1,0:T(8,128)(2,1)} %param.3), channel_id=1, source_target_pairs={{0,8},{4,12},{8,0},{12,4},{1,9},{5,13},{9,1},{13,5},{2,10},{6,14},... | collective-permute-start | bytes 2359304 | tf_op jit(solution)/shard_map/ppermute | solution.py:105
  3.0 17.8 %collective-permute-start = (bf16[8,64,768]{2,1,0:T(8,128)(2,1)}, bf16[8,64,768]{2,1,0:T(8,128)(2,1)S(1)}, u32[]{:S(2)}, u32[]{:S(2)}) collective-permute-start(bf16[8,64,768]{2,1,0:T(8,128)(2,1)} %param.3), channel_id=1, source_target_pairs={{0,4},{4,0},{8,12},{12,8},{1,5},{5,1},{9,13},{13,9},{2,6},{6,2},{1... | collective-permute-start | bytes 2359304 | tf_op jit(solution)/shard_map/ppermute | solution.py:105
  20.7 2.3 collective-permute-start.2
  42.9 26.1 %collective-permute-start.3 = (bf16[1024,512]{1,0:T(8,128)(2,1)S(1)}, bf16[1024,512]{1,0:T(8,128)(2,1)S(1)}, u32[]{:S(2)}, u32[]{:S(2)}) collective-permute-start(bf16[1024,512]{1,0:T(8,128)(2,1)S(1)} %dynamic-slice_bitcast_fusion.3), channel_id=1, source_target_pairs={{0,16},{16,0},{1,17},{17,1},{2,18},{18,2},{3,19},{19,3},{4,20},{20... | collective-permute-start | bytes 3145736 | tf_op jit(solution)/shard_map/ppermute | solution.py:105
  63.7 27.7 %collective-permute-start.6 = (bf16[1024,512]{1,0:T(8,128)(2,1)S(1)}, bf16[1024,512]{1,0:T(8,128)(2,1)S(1)}, u32[]{:S(2)}, u32[]{:S(2)}) collective-permute-start(bf16[1024,512]{1,0:T(8,128)(2,1)S(1)} %dynamic-slice_bitcast_fusion.2), channel_id=1, source_target_pairs={{0,16},{16,0},{1,17},{17,1},{2,18},{18,2},{3,19},{19,3},{4,20},{20... | collective-permute-start | bytes 3145736 | tf_op jit(solution)/shard_map/ppermute | solution.py:105
  69.3 22.1 %collective-permute-start.5 = (bf16[2,256,512]{2,1,0:T(8,128)(2,1)S(1)}, bf16[2,256,512]{2,1,0:T(8,128)(2,1)S(1)}, u32[]{:S(2)}, u32[]{:S(2)}) collective-permute-start(bf16[2,256,512]{2,1,0:T(8,128)(2,1)S(1)} %dynamic-slice_bitcast_fusion.7), channel_id=1, source_target_pairs={{0,1},{1,0},{2,3},{3,2},{4,5},{5,4},{6,7},{7,6},{8,9},{9,8},{10,11... | collective-permute-start | bytes 1572872 | tf_op jit(solution)/shard_map/ppermute | solution.py:105
  91.5 13.6 %collective-permute-start.7 = (bf16[256,512]{1,0:T(8,128)(2,1)S(1)}, bf16[256,512]{1,0:T(8,128)(2,1)S(1)}, u32[]{:S(2)}, u32[]{:S(2)}) collective-permute-start(bf16[256,512]{1,0:T(8,128)(2,1)S(1)} %dynamic-slice_bitcast_fusion.10), channel_id=1, source_target_pairs={{0,2},{1,3},{2,0},{3,1},{4,6},{5,7},{6,4},{7,5},{8,10},{9,11},{10,... | collective-permute-start | bytes 786440 | tf_op jit(solution)/shard_map/ppermute | solution.py:105
  95.3 27.2 %collective-permute-start.10 = (bf16[2,256,512]{2,1,0:T(8,128)(2,1)}, bf16[2,256,512]{2,1,0:T(8,128)(2,1)}, u32[]{:S(2)}, u32[]{:S(2)}) collective-permute-start(bf16[2,256,512]{2,1,0:T(8,128)(2,1)} %dynamic-slice_bitcast_fusion.6), channel_id=1, source_target_pairs={{0,1},{1,0},{2,3},{3,2},{4,5},{5,4},{6,7},{7,6},{8,9},{9,8},{10,11... | collective-permute-start | bytes 1572872 | tf_op jit(solution)/shard_map/ppermute | solution.py:105
  105.3 13.8 %collective-permute-start.8 = (bf16[256,512]{1,0:T(8,128)(2,1)S(1)}, bf16[256,512]{1,0:T(8,128)(2,1)}, u32[]{:S(2)}, u32[]{:S(2)}) collective-permute-start(bf16[256,512]{1,0:T(8,128)(2,1)S(1)} %multiply_convert_fusion.2), channel_id=1, source_target_pairs={{0,2},{1,3},{2,0},{3,1},{4,6},{5,7},{6,4},{7,5},{8,10},{9,11},{10,... | collective-permute-start | bytes 786440 | tf_op jit(solution)/shard_map/ppermute | solution.py:105
  105.4 36.6 %collective-permute-start.4 = (bf16[1024,512]{1,0:T(8,128)(2,1)}, bf16[1024,512]{1,0:T(8,128)(2,1)}, u32[]{:S(2)}, u32[]{:S(2)}) collective-permute-start(bf16[1024,512]{1,0:T(8,128)(2,1)} %dynamic-slice_bitcast_fusion.1), channel_id=1, source_target_pairs={{0,16},{16,0},{1,17},{17,1},{2,18},{18,2},{3,19},{19,3},{4,20},{20... | collective-permute-start | bytes 3145736 | tf_op jit(solution)/shard_map/ppermute | solution.py:105
  121.0 19.5 %collective-permute-start.9 = (bf16[2,256,512]{2,1,0:T(8,128)(2,1)}, bf16[2,256,512]{2,1,0:T(8,128)(2,1)}, u32[]{:S(2)}, u32[]{:S(2)}) collective-permute-start(bf16[2,256,512]{2,1,0:T(8,128)(2,1)} %maximum_select_fusion.9), channel_id=1, source_target_pairs={{0,1},{1,0},{2,3},{3,2},{4,5},{5,4},{6,7},{7,6},{8,9},{9,8},{10,11... | collective-permute-start | bytes 1572872 | tf_op jit(solution)/shard_map/ppermute | solution.py:105
  123.7 0.8 copy-start.3
  124.5 14.8 %collective-permute-start.11 = (bf16[256,512]{1,0:T(8,128)(2,1)S(1)}, bf16[256,512]{1,0:T(8,128)(2,1)}, u32[]{:S(2)}, u32[]{:S(2)}) collective-permute-start(bf16[256,512]{1,0:T(8,128)(2,1)S(1)} %dynamic-slice_bitcast_fusion.9), channel_id=1, source_target_pairs={{0,2},{1,3},{2,0},{3,1},{4,6},{5,7},{6,4},{7,5},{8,10},{9,11},{10,... | collective-permute-start | bytes 786440 | tf_op jit(solution)/shard_map/ppermute | solution.py:105
  143.5 22.6 %collective-permute-start.12 = (bf16[2,256,512]{2,1,0:T(8,128)(2,1)S(1)}, bf16[2,256,512]{2,1,0:T(8,128)(2,1)S(1)}, u32[]{:S(2)}, u32[]{:S(2)}) collective-permute-start(bf16[2,256,512]{2,1,0:T(8,128)(2,1)S(1)} %dynamic-slice_bitcast_fusion.5), channel_id=1, source_target_pairs={{0,1},{1,0},{2,3},{3,2},{4,5},{5,4},{6,7},{7,6},{8,9},{9,8},{10,11... | collective-permute-start | bytes 1572872 | tf_op jit(solution)/shard_map/ppermute | solution.py:105
  147.9 16.0 %collective-permute-start.17 = (bf16[256,512]{1,0:T(8,128)(2,1)S(1)}, bf16[256,512]{1,0:T(8,128)(2,1)S(1)}, u32[]{:S(2)}, u32[]{:S(2)}) collective-permute-start(bf16[256,512]{1,0:T(8,128)(2,1)S(1)} %multiply_convert_fusion.1), channel_id=1, source_target_pairs={{0,2},{1,3},{2,0},{3,1},{4,6},{5,7},{6,4},{7,5},{8,10},{9,11},{10,... | collective-permute-start | bytes 786440 | tf_op jit(solution)/shard_map/ppermute | solution.py:105
  148.5 39.1 %collective-permute-start.20 = (bf16[1024,512]{1,0:T(8,128)(2,1)S(1)}, bf16[1024,512]{1,0:T(8,128)(2,1)}, u32[]{:S(2)}, u32[]{:S(2)}) collective-permute-start(bf16[1024,512]{1,0:T(8,128)(2,1)S(1)} %bitcast.140), channel_id=1, source_target_pairs={{0,16},{16,0},{1,17},{17,1},{2,18},{18,2},{3,19},{19,3},{4,20},{20... | collective-permute-start | bytes 3145736 | tf_op jit(solution)/shard_map/ppermute | solution.py:105
  164.8 20.9 %collective-permute-start.18 = (bf16[2,256,512]{2,1,0:T(8,128)(2,1)}, bf16[2,256,512]{2,1,0:T(8,128)(2,1)S(1)}, u32[]{:S(2)}, u32[]{:S(2)}) collective-permute-start(bf16[2,256,512]{2,1,0:T(8,128)(2,1)} %maximum_select_fusion.12), channel_id=1, source_target_pairs={{0,1},{1,0},{2,3},{3,2},{4,5},{5,4},{6,7},{7,6},{8,9},{9,8},{10,11... | collective-permute-start | bytes 1572872 | tf_op jit(solution)/shard_map/ppermute | solution.py:105
  166.3 14.8 %collective-permute-start.13 = (bf16[256,512]{1,0:T(8,128)(2,1)S(1)}, bf16[256,512]{1,0:T(8,128)(2,1)}, u32[]{:S(2)}, u32[]{:S(2)}) collective-permute-start(bf16[256,512]{1,0:T(8,128)(2,1)S(1)} %dynamic-slice_bitcast_fusion.8), channel_id=1, source_target_pairs={{0,2},{1,3},{2,0},{3,1},{4,6},{5,7},{6,4},{7,5},{8,10},{9,11},{10,... | collective-permute-start | bytes 786440 | tf_op jit(solution)/shard_map/ppermute | solution.py:105
  182.2 14.4 %collective-permute-start.14 = (bf16[256,512]{1,0:T(8,128)(2,1)S(1)}, bf16[256,512]{1,0:T(8,128)(2,1)S(1)}, u32[]{:S(2)}, u32[]{:S(2)}) collective-permute-start(bf16[256,512]{1,0:T(8,128)(2,1)S(1)} %multiply_convert_fusion), channel_id=1, source_target_pairs={{0,2},{1,3},{2,0},{3,1},{4,6},{5,7},{6,4},{7,5},{8,10},{9,11},{10,... | collective-permute-start | bytes 786440 | tf_op jit(solution)/shard_map/ppermute | solution.py:105
  186.0 32.3 %collective-permute-start.19 = (bf16[1024,512]{1,0:T(8,128)(2,1)S(1)}, bf16[1024,512]{1,0:T(8,128)(2,1)S(1)}, u32[]{:S(2)}, u32[]{:S(2)}) collective-permute-start(bf16[1024,512]{1,0:T(8,128)(2,1)S(1)} %bitcast.142), channel_id=1, source_target_pairs={{0,16},{16,0},{1,17},{17,1},{2,18},{18,2},{3,19},{19,3},{4,20},{20... | collective-permute-start | bytes 3145736 | tf_op jit(solution)/shard_map/ppermute | solution.py:105
  196.7 19.9 %collective-permute-start.15 = (bf16[2,256,512]{2,1,0:T(8,128)(2,1)S(1)}, bf16[2,256,512]{2,1,0:T(8,128)(2,1)S(1)}, u32[]{:S(2)}, u32[]{:S(2)}) collective-permute-start(bf16[2,256,512]{2,1,0:T(8,128)(2,1)S(1)} %maximum_select_fusion.10), channel_id=1, source_target_pairs={{0,1},{1,0},{2,3},{3,2},{4,5},{5,4},{6,7},{7,6},{8,9},{9,8},{10,11... | collective-permute-start | bytes 1572872 | tf_op jit(solution)/shard_map/ppermute | solution.py:105
  216.7 23.4 %collective-permute-start.16 = (bf16[1024,512]{1,0:T(8,128)(2,1)S(1)}, bf16[1024,512]{1,0:T(8,128)(2,1)S(1)}, u32[]{:S(2)}, u32[]{:S(2)}) collective-permute-start(bf16[1024,512]{1,0:T(8,128)(2,1)S(1)} %bitcast.138), channel_id=1, source_target_pairs={{0,16},{16,0},{1,17},{17,1},{2,18},{18,2},{3,19},{19,3},{4,20},{20... | collective-permute-start | bytes 3145736 | tf_op jit(solution)/shard_map/ppermute | solution.py:105
  254.4 1.4 copy-start
  257.0 2.9 collective-permute-start.21
  261.4 1.4 copy-start.1
  262.8 14.0 %collective-permute-start.22 = (bf16[512,512]{1,0:T(8,128)(2,1)S(1)}, bf16[512,512]{1,0:T(8,128)(2,1)S(1)}, u32[]{:S(2)}, u32[]{:S(2)}) collective-permute-start(bf16[512,512]{1,0:T(8,128)(2,1)S(1)} %fusion.6), channel_id=1, source_target_pairs={{0,8},{4,12},{8,0},{12,4},{1,9},{5,13},{9,1},{13,5},{2,10},{6,14},... | collective-permute-start | bytes 1572872 | tf_op jit(solution)/shard_map/ppermute | solution.py:105
  276.7 0.8 copy-start.4
  277.6 2.0 collective-permute-start.23
  277.6 3.6 %copy-start.2 = (bf16[8,64,768]{2,1,0:T(8,128)(2,1)S(1)}, bf16[8,64,768]{2,1,0:T(8,128)(2,1)}, u32[]{:S(2)}) copy-start(bf16[8,64,768]{2,1,0:T(8,128)(2,1)} %param.3) | copy-start | bytes 2359300
  279.7 8.5 %collective-permute-start.24 = (bf16[512,256]{1,0:T(8,128)(2,1)S(1)}, bf16[512,256]{1,0:T(8,128)(2,1)S(1)}, u32[]{:S(2)}, u32[]{:S(2)}) collective-permute-start(bf16[512,256]{1,0:T(8,128)(2,1)S(1)} %fusion.8), channel_id=1, source_target_pairs={{0,8},{4,12},{8,0},{12,4},{1,9},{5,13},{9,1},{13,5},{2,10},{6,14},... | collective-permute-start | bytes 786440 | tf_op jit(solution)/shard_map/ppermute | solution.py:105
